TPU v7x, 256 devices: a whole 4x4x8 slice. The times are simulated.
256 devices in a mesh: blk: 64 (over x, z, core), rep: 4 (over y).
Axes of the slice: x: 4, y: 4, z: 8, core: 2. Of those that a mesh axis runs over, the one named last changes fastest.
Arguments:
- source: bfloat16 [512, 512, 256], P('blk'), may hold values from -2 to 2
- targets: bfloat16 [256, 512, 256], P('blk', 'rep'), may hold values from -2 to 2
- log_a: float32 [512, 512], P('blk'), may hold values from -2 to 2
- log_b: float32 [256, 512], P('blk', 'rep'), may hold values from -2 to 2
- pair_source: int32 [64, 48], replicated, may hold values from 0 to 7, as said below
- pair_target: int32 [64, 48], replicated, may hold values from 0 to 255, as said below
- pair_count: int32 [64], replicated, may hold values from 24 to 48, as said below
Outputs:
- source_potential: float32 [512, 512], P('blk')
- target_potential: float32 [256, 512], P('blk', 'rep')
Inputs may be any that keep to these rules, and one draw needn't show every extreme that they name: Owner o has pair_count[o] live pairs; one owner has exactly 48. `pair_source`: every one of an owner's 8 source blocks is named by one of its live pairs. Slots past the live count hold valid numbers and are unused. `pair_target`: target block t belongs to owner t // 4. An owner's live pairs name at most one block of each target owner, no live pair repeats within an owner, and every target block is named by some live pair. Slots past the live count hold valid numbers and are unused.
All inputs are finite; a program needn't handle non-finite values.
Results may differ from a plain program's by a relative error of at most 0.0003.
Values may be sent and summed in bfloat16 or wider, within the bound.
No kernel may reach another device: no remote copies, remote signals or barrier semaphores. Data moves between devices by JAX's collectives and lax.ppermute only.
A program may use at most 128 MiB of HBM per device.

v0:
```python
import jax
import jax.numpy as jnp
from jax import lax
from jax.sharding import PartitionSpec as P

ITERS = 2


epsilon = 0.1
floor_value = -1e30


def absorb(running_peak, hit_table, tile_max, tile_sum):
    hit_mask = hit_table[:, :, None]
    candidate = jnp.max(jnp.where(hit_mask, tile_max[:, None, :], floor_value), axis=0)
    raised = jnp.maximum(running_peak, candidate)
    picked = jnp.sum(jnp.where(hit_mask, raised[None], 0.0), axis=1)
    increment = jnp.sum(
        jnp.where(hit_mask, (tile_sum * jnp.exp(tile_max - picked))[:, None, :], 0.0), axis=0
    )
    return (raised, increment)


def per_device(source, targets, log_a, log_b, pair_source, pair_target, pair_count):
    self_index = lax.axis_index("blk")
    owners = lax.axis_size("blk")
    local_blocks = targets.shape[0]
    source_blocks = source.shape[0]
    quarter = targets.shape[1]
    live_slot = lax.broadcasted_iota(jnp.int32, pair_target.shape, 1) < pair_count[:, None]
    asked_here = live_slot & (pair_target // local_blocks == self_index)
    wanted = jnp.max(jnp.where(asked_here, pair_target % local_blocks, -1), axis=1)
    selector = wanted[:, None] == jnp.arange(local_blocks, dtype=jnp.int32)[None, :]
    my_source = lax.dynamic_index_in_dim(pair_source, self_index, 0, keepdims=False)
    my_target = lax.dynamic_index_in_dim(pair_target, self_index, 0, keepdims=False)
    my_count = lax.dynamic_index_in_dim(pair_count, self_index, 0, keepdims=False)
    peer_slots = my_target // local_blocks
    fetched = lax.all_gather(targets, "blk", axis=0, tiled=True)
    slot_count = my_source.shape[0]
    valid_slot = jnp.arange(slot_count, dtype=jnp.int32) < my_count
    left_rows = jnp.take(source, my_source, axis=0)
    right_rows = jnp.take(fetched, my_target, axis=0)
    tiles = jnp.einsum("sae,sbe->sab", left_rows, right_rows, preferred_element_type=jnp.float32)
    row_hits = valid_slot[:, None] & (
        my_source[:, None] == jnp.arange(source_blocks, dtype=jnp.int32)[None, :]
    )
    column_hits = valid_slot[:, None] & (
        peer_slots[:, None] == jnp.arange(owners, dtype=jnp.int32)[None, :]
    )
    near_potential = jnp.zeros((fetched.shape[0], quarter), jnp.float32)
    source_potential = jnp.zeros(log_a.shape, jnp.float32)
    target_potential = jnp.zeros(log_b.shape, jnp.float32)
    chosen_mask = selector[:, :, None]
    for iteration in range(ITERS):
        if iteration > 0:
            near_potential = lax.all_gather(target_potential, "blk", axis=0, tiled=True)
        row_scores = (jnp.take(near_potential, my_target, axis=0)[:, None, :] + tiles) / epsilon
        row_tile_max = jnp.max(row_scores, axis=2)
        row_tile_sum = jnp.sum(jnp.exp(row_scores - row_tile_max[:, :, None]), axis=2)
        row_initial_peak = jnp.full(log_a.shape, floor_value, jnp.float32)
        row_peak, row_total = absorb(row_initial_peak, row_hits, row_tile_max, row_tile_sum)
        highest = lax.pmax(row_peak, "rep")
        row_total = lax.psum(row_total * jnp.exp(row_peak - highest), "rep")
        row_peak = highest
        source_potential = epsilon * log_a - epsilon * (row_peak + jnp.log(row_total))
        scores = (jnp.take(source_potential, my_source, axis=0)[:, :, None] + tiles) / epsilon
        tile_max = jnp.max(scores, axis=1)
        tile_sum = jnp.sum(jnp.exp(scores - tile_max[:, None, :]), axis=1)
        initial_peak = jnp.full((owners, quarter), floor_value, jnp.float32)
        column_peak, column_total = absorb(initial_peak, column_hits, tile_max, tile_sum)
        back_peak, back_total = (
            lax.all_to_all(column_peak, "blk", split_axis=0, concat_axis=0, tiled=True),
            lax.all_to_all(column_total, "blk", split_axis=0, concat_axis=0, tiled=True),
        )
        column_top = jnp.max(jnp.where(chosen_mask, back_peak[:, None, :], floor_value), axis=0)
        column_mass = jnp.sum(
            jnp.where(
                chosen_mask,
                back_total[:, None, :] * jnp.exp(back_peak[:, None, :] - column_top[None]),
                0.0,
            ),
            axis=0,
        )
        target_potential = epsilon * log_b - epsilon * (column_top + jnp.log(column_mass))
    return (source_potential, target_potential)


def solution(mesh):
    in_specs = (
        P("blk", None, None),
        P("blk", "rep", None),
        P("blk", None),
        P("blk", "rep"),
        P(),
        P(),
        P(),
    )
    out_specs = (P("blk", None), P("blk", "rep"))
    return jax.shard_map(
        per_device, mesh=mesh, in_specs=in_specs, out_specs=out_specs, check_vma=False
    )
```

profile of v0, /device:TPU:1, one launch (start us, length us, event | category | flops | bytes accessed | tf_op | source)
XLA Modules:
  0.0 374.4 jit_solution(7775301781460707736)
XLA Ops:
  7.2 0.0 copy-start
  7.2 0.0 all-gather.3.cloned.1.call-start
  7.2 0.7 all-gather.3.cloned.1.call-update
  7.9 1.2 dynamic_slice.11
  9.2 0.9 dynamic-slice_reduce_fusion
  10.1 0.6 gather_fusion.2
  10.7 0.9 dynamic-slice_reduce_fusion.1
  11.7 0.0 copy-done
  11.7 0.0 copy-start.2
  11.7 0.0 copy-start.5
  11.7 6.1 %gather_fusion = bf16[48,512,256]{2,1,0:T(8,128)(2,1)} fusion(bf16[8,512,256]{2,1,0:T(8,128)(2,1)S(1)} %copy-done, s32[1024]{0:T(1024)S(1)} %pad_clamp_fusion.2), kind=kCustom, calls=%fused_computation.4 | custom fusion | bytes 25166016 | tf_op jit(solution)/shard_map/jit(_take)/gather | solution.py:41
  17.8 0.6 iota_compare_fusion.4
  18.6 0.1 fusion.14
  18.6 0.1 fusion.17
  18.7 0.1 broadcast_select_fusion.3
  18.8 95.9 %all-gather.3.cloned.1.call-done = bf16[256,128,256]{2,1,0:T(8,128)(2,1)} async-done(((bf16[4,128,256]{2,1,0:T(8,128)(2,1)}), bf16[256,128,256]{2,1,0:T(8,128)(2,1)}) %all-gather.3.cloned.1.call-update) | async-done | bytes 16777232 | tf_op jit(solution)/shard_map/all_gather | solution.py:38
  114.7 8.3 %gather_fusion.1 = bf16[48,128,256]{2,1,0:T(8,128)(2,1)} fusion(bf16[256,128,256]{2,1,0:T(8,128)(2,1)} %all-gather.3.cloned.1.call-done, s32[1024]{0:T(1024)S(1)} %pad_clamp_fusion.1), kind=kCustom, calls=%fused_computation.5 | custom fusion | bytes 6291648 | tf_op jit(solution)/shard_map/jit(_take)/gather | solution.py:42
  123.0 10.5 %fusion.3 = (f32[48,512]{1,0:T(8,128)S(1)}, f32[48,512,128]{2,1,0:T(8,128)}) fusion(f32[48,128]{1,0:T(8,128)S(1)} %broadcast_select_fusion.3, bf16[48,128,256]{2,1,0:T(8,128)(2,1)} %gather_fusion.1, pred[48]{0:T(512)(128)(4,1)S(1)} %get-tuple-element.8, bf16[48,512,256]{2,1,0:T(8,128)(2,1)} %gather_fusion, pred[48]{0:T(512)(128)(4,1)S(1)} %get-tuple-element.9), kind=kOutput, calls=%fused_computation.17 | convolution fusion | flops 1627889664 | bytes 28434528 | tf_op jit(solution)/shard_map/sae,sbe->sab/dot_general | solution.py:43
  133.5 0.1 select_reduce_fusion.11
  133.7 13.1 %pmax.14 = f32[8,512]{1,0:T(8,128)S(1)} all-reduce(f32[8,512]{1,0:T(8,128)S(1)} %broadcast_maximum_fusion.3), channel_id=1, replica_groups=mesh['blk'=64,'rep'=4] {'rep'}, use_global_device_ids=true, to_apply=%region_3.5 | all-reduce | flops 4096 | bytes 32768 | tf_op jit(solution)/shard_map/pmax | solution.py:62
  146.8 0.3 select_reduce_fusion.10
  147.1 8.8 %exponential_reduce_fusion.3 = f32[48,512]{1,0:T(8,128)S(1)} fusion(f32[48,512,128]{2,1,0:T(8,128)} %get-tuple-element.7, f32[48,512]{1,0:T(8,128)S(1)} %get-tuple-element.6, f32[48,128]{1,0:T(8,128)S(1)} %broadcast_select_fusion.3), kind=kLoop, calls=%fused_computation.12 | loop fusion | flops 12558336 | bytes 12804096 | tf_op jit(solution)/shard_map/reduce_sum | solution.py:59
  155.9 0.1 select_reduce_fusion.9
  156.1 10.8 %psum.14 = f32[8,512]{1,0:T(8,128)S(1)} all-reduce(f32[8,512]{1,0:T(8,128)S(1)} %exponential_multiply_fusion.5), channel_id=1, replica_groups=mesh['blk'=64,'rep'=4] {'rep'}, use_global_device_ids=true, to_apply=%region_7.9 | all-reduce | flops 4096 | bytes 32768 | tf_op jit(solution)/shard_map/psum | solution.py:63
  166.9 0.6 gather_fusion.3
  167.5 0.1 broadcast_select_fusion.1
  167.6 7.6 %fusion.4 = f32[48,128]{1,0:T(8,128)S(1)} fusion(f32[48,512,128]{2,1,0:T(8,128)} %get-tuple-element.7, f32[48,512]{1,0:T(8,128)S(1)} %broadcast_select_fusion.1), kind=kLoop, calls=%fused_computation.18 | loop fusion | flops 9431040 | bytes 12705792 | tf_op jit(solution)/shard_map/reduce_max | solution.py:67
  175.2 8.5 %exponential_reduce_fusion.2 = f32[48,128]{1,0:T(8,128)S(1)} fusion(f32[48,512,128]{2,1,0:T(8,128)} %get-tuple-element.7, f32[48,128]{1,0:T(8,128)S(1)} %fusion.4, f32[48,512]{1,0:T(8,128)S(1)} %broadcast_select_fusion.1), kind=kLoop, calls=%fused_computation.10 | loop fusion | flops 12576768 | bytes 12730368 | tf_op jit(solution)/shard_map/reduce_sum | solution.py:68
  183.7 0.6 select_reduce_fusion.5
  184.3 0.6 broadcast_maximum_fusion.1
  184.9 1.3 select_reduce_fusion.4
  186.2 13.2 %all-to-all-start = ((f32[64,1,128]{2,1,0:T(1,128)}), f32[64,1,128]{2,1,0:T(1,128)S(1)}, u32[]{:S(2)}, u32[]{:S(2)}) async-start(f32[64,1,128]{2,1,0:T(1,128)} %bitcast.4), calls=%async_computation | async-start | bytes 65536 | tf_op jit(solution)/shard_map/all_to_all | solution.py:72
  199.5 1.2 select_reduce_fusion.3
  200.7 8.1 %all-to-all-done = f32[64,1,128]{2,1,0:T(1,128)S(1)} async-done(((f32[64,1,128]{2,1,0:T(1,128)}), f32[64,1,128]{2,1,0:T(1,128)S(1)}, u32[]{:S(2)}, u32[]{:S(2)}) %all-to-all-start) | async-done | bytes 32800 | tf_op jit(solution)/shard_map/all_to_all | solution.py:72
  208.8 4.7 %all-to-all-start.1 = ((f32[64,1,128]{2,1,0:T(1,128)}), f32[64,1,128]{2,1,0:T(1,128)S(1)}, u32[]{:S(2)}, u32[]{:S(2)}) async-start(f32[64,1,128]{2,1,0:T(1,128)} %bitcast.7), calls=%async_computation.1 | async-start | bytes 65536 | tf_op jit(solution)/shard_map/all_to_all | solution.py:73
  213.5 0.1 select_reduce_fusion.15
  213.6 9.3 %all-to-all-done.1 = f32[64,1,128]{2,1,0:T(1,128)S(1)} async-done(((f32[64,1,128]{2,1,0:T(1,128)}), f32[64,1,128]{2,1,0:T(1,128)S(1)}, u32[]{:S(2)}, u32[]{:S(2)}) %all-to-all-start.1) | async-done | bytes 32800 | tf_op jit(solution)/shard_map/all_to_all | solution.py:73
  222.9 0.1 select_reduce_fusion.14
  223.0 48.1 %all-gather = f32[64,4,128]{2,1,0:T(4,128)S(1)} all-gather(f32[1,4,128]{2,1,0:T(4,128)S(1)} %subtract_bitcast_fusion), channel_id=1, replica_groups=mesh['blk'=64,'rep'=4] {'blk'}, dimensions={0}, use_global_device_ids=true | all-gather | bytes 133120 | tf_op jit(solution)/shard_map/all_gather | solution.py:56
  271.1 0.6 gather_fusion.4
  271.7 0.1 broadcast_select_fusion.2
  271.8 7.9 %fusion.5 = f32[48,512]{1,0:T(8,128)S(1)} fusion(f32[48,512,128]{2,1,0:T(8,128)} %get-tuple-element.7, f32[48,128]{1,0:T(8,128)S(1)} %broadcast_select_fusion.2), kind=kLoop, calls=%fused_computation.19 | loop fusion | flops 9412608 | bytes 12705792 | tf_op jit(solution)/shard_map/reduce_max | solution.py:58
  279.7 0.1 select_reduce_fusion.8
  279.8 8.8 %exponential_reduce_fusion.1 = f32[48,512]{1,0:T(8,128)S(1)} fusion(f32[48,512,128]{2,1,0:T(8,128)} %get-tuple-element.7, f32[48,512]{1,0:T(8,128)S(1)} %fusion.5, f32[48,128]{1,0:T(8,128)S(1)} %broadcast_select_fusion.2), kind=kLoop, calls=%fused_computation.8 | loop fusion | flops 12558336 | bytes 12804096 | tf_op jit(solution)/shard_map/reduce_sum | solution.py:59
  288.6 11.7 %pmax.15 = f32[8,512]{1,0:T(8,128)S(1)} all-reduce(f32[8,512]{1,0:T(8,128)S(1)} %broadcast_maximum_fusion.2), channel_id=1, replica_groups=mesh['blk'=64,'rep'=4] {'rep'}, use_global_device_ids=true, to_apply=%region_17.20 | all-reduce | flops 4096 | bytes 32768 | tf_op jit(solution)/shard_map/pmax | solution.py:62
  300.3 0.3 select_reduce_fusion.7
  300.6 0.1 select_reduce_fusion.6
  300.8 10.8 %psum.15 = f32[8,512]{1,0:T(8,128)S(1)} all-reduce(f32[8,512]{1,0:T(8,128)S(1)} %exponential_multiply_fusion.4), channel_id=1, replica_groups=mesh['blk'=64,'rep'=4] {'rep'}, use_global_device_ids=true, to_apply=%region_21.24 | all-reduce | flops 4096 | bytes 32768 | tf_op jit(solution)/shard_map/psum | solution.py:63
  311.6 0.0 copy-start.1
  311.6 0.6 gather_fusion.5
  312.2 0.1 broadcast_select_fusion
  312.3 7.6 %fusion.6 = f32[48,128]{1,0:T(8,128)S(1)} fusion(f32[48,512,128]{2,1,0:T(8,128)} %get-tuple-element.7, f32[48,512]{1,0:T(8,128)S(1)} %broadcast_select_fusion), kind=kLoop, calls=%fused_computation.20 | loop fusion | flops 9431040 | bytes 12705792 | tf_op jit(solution)/shard_map/reduce_max | solution.py:67
  319.9 0.6 select_reduce_fusion.2
  320.5 8.5 %exponential_reduce_fusion = f32[48,128]{1,0:T(8,128)S(1)} fusion(f32[48,512,128]{2,1,0:T(8,128)} %get-tuple-element.7, f32[48,128]{1,0:T(8,128)S(1)} %fusion.6, f32[48,512]{1,0:T(8,128)S(1)} %broadcast_select_fusion), kind=kLoop, calls=%fused_computation.6 | loop fusion | flops 12576768 | bytes 12730368 | tf_op jit(solution)/shard_map/reduce_sum | solution.py:68
  329.0 0.6 broadcast_maximum_fusion
  329.6 1.3 select_reduce_fusion.1
  331.0 12.5 %all-to-all-start.2 = ((f32[64,1,128]{2,1,0:T(1,128)}), f32[64,1,128]{2,1,0:T(1,128)S(1)}, u32[]{:S(2)}, u32[]{:S(2)}) async-start(f32[64,1,128]{2,1,0:T(1,128)} %bitcast.12), calls=%async_computation.2 | async-start | bytes 65536 | tf_op jit(solution)/shard_map/all_to_all | solution.py:72
  343.5 1.2 select_reduce_fusion
  344.7 8.1 %all-to-all-done.2 = f32[64,1,128]{2,1,0:T(1,128)S(1)} async-done(((f32[64,1,128]{2,1,0:T(1,128)}), f32[64,1,128]{2,1,0:T(1,128)S(1)}, u32[]{:S(2)}, u32[]{:S(2)}) %all-to-all-start.2) | async-done | bytes 32800 | tf_op jit(solution)/shard_map/all_to_all | solution.py:72
  352.8 4.7 %all-to-all-start.3 = ((f32[64,1,128]{2,1,0:T(1,128)}), f32[64,1,128]{2,1,0:T(1,128)S(1)}, u32[]{:S(2)}, u32[]{:S(2)}) async-start(f32[64,1,128]{2,1,0:T(1,128)} %bitcast.15), calls=%async_computation.3 | async-start | bytes 65536 | tf_op jit(solution)/shard_map/all_to_all | solution.py:73
  357.4 0.1 select_reduce_fusion.13
  357.6 9.3 %all-to-all-done.3 = f32[64,1,128]{2,1,0:T(1,128)S(1)} async-done(((f32[64,1,128]{2,1,0:T(1,128)}), f32[64,1,128]{2,1,0:T(1,128)S(1)}, u32[]{:S(2)}, u32[]{:S(2)}) %all-to-all-start.3) | async-done | bytes 32800 | tf_op jit(solution)/shard_map/all_to_all | solution.py:73
  366.8 0.1 select_reduce_fusion.12
  366.9 0.6 multiply_subtract_fusion.2
  (30 shorter events, 0.3 us)
Async XLA Ops:
  7.2 4.5 %copy-start = (bf16[8,512,256]{2,1,0:T(8,128)(2,1)S(1)}, bf16[8,512,256]{2,1,0:T(8,128)(2,1)}, u32[]{:S(2)}) copy-start(bf16[8,512,256]{2,1,0:T(8,128)(2,1)} %param.11) | copy-start | bytes 6291460
  7.2 107.6 %all-gather.3.cloned.1.call-start = ((), (), s32[]{:S(2)}) async-start(), calls=%async_computation.4 | async-start | bytes 17039360 | tf_op jit(solution)/shard_map/all_gather | solution.py:38
  11.7 6.8 %copy-start.2 = (s32[64,48]{0,1:T(8,128)S(1)}, s32[64,48]{0,1:T(8,128)}, u32[]{:S(2)}) copy-start(s32[64,48]{0,1:T(8,128)} %param.16) | copy-start | bytes 36868
  11.7 6.8 %copy-start.5 = (s32[64]{0:T(128)S(1)}, s32[64]{0:T(128)}, u32[]{:S(2)}) copy-start(s32[64]{0:T(128)} %param.17) | copy-start | bytes 772
  133.5 33.4 %copy-start.3 = (f32[8,512]{1,0:T(8,128)S(1)}, f32[8,512]{1,0:T(8,128)}, u32[]{:S(2)}) copy-start(f32[8,512]{1,0:T(8,128)} %param.13) | copy-start | bytes 49156
  167.6 55.4 %copy-start.4 = (f32[4,128]{1,0:T(4,128)S(1)}, f32[4,128]{1,0:T(4,128)}, u32[]{:S(2)}) copy-start(f32[4,128]{1,0:T(4,128)} %param.14) | copy-start | bytes 6148
  186.2 22.5 %all-to-all-start = ((f32[64,1,128]{2,1,0:T(1,128)}), f32[64,1,128]{2,1,0:T(1,128)S(1)}, u32[]{:S(2)}, u32[]{:S(2)}) async-start(f32[64,1,128]{2,1,0:T(1,128)} %bitcast.4), calls=%async_computation | async-start | bytes 65536 | tf_op jit(solution)/shard_map/all_to_all | solution.py:72
  208.8 14.1 %all-to-all-start.1 = ((f32[64,1,128]{2,1,0:T(1,128)}), f32[64,1,128]{2,1,0:T(1,128)S(1)}, u32[]{:S(2)}, u32[]{:S(2)}) async-start(f32[64,1,128]{2,1,0:T(1,128)} %bitcast.7), calls=%async_computation.1 | async-start | bytes 65536 | tf_op jit(solution)/shard_map/all_to_all | solution.py:73
  311.6 17.4 %copy-start.1 = (f32[8,512]{1,0:T(8,128)}, f32[8,512]{1,0:T(8,128)S(1)}, u32[]{:S(2)}) copy-start(f32[8,512]{1,0:T(8,128)S(1)} %multiply_subtract_fusion) | copy-start | bytes 49156
  331.0 21.8 %all-to-all-start.2 = ((f32[64,1,128]{2,1,0:T(1,128)}), f32[64,1,128]{2,1,0:T(1,128)S(1)}, u32[]{:S(2)}, u32[]{:S(2)}) async-start(f32[64,1,128]{2,1,0:T(1,128)} %bitcast.12), calls=%async_computation.2 | async-start | bytes 65536 | tf_op jit(solution)/shard_map/all_to_all | solution.py:72
  352.8 14.1 %all-to-all-start.3 = ((f32[64,1,128]{2,1,0:T(1,128)}), f32[64,1,128]{2,1,0:T(1,128)S(1)}, u32[]{:S(2)}, u32[]{:S(2)}) async-start(f32[64,1,128]{2,1,0:T(1,128)} %bitcast.15), calls=%async_computation.3 | async-start | bytes 65536 | tf_op jit(solution)/shard_map/all_to_all | solution.py:73
Sparse Core Ops, SparseCore 0:
  10.8 103.8 all-gather.2
where the time goes:
time: 375 us; the launch traced here: 374 us
  waiting for transfers between devices  131 us (35%)
  blocking collectives  94.5 us (25%)
  other arithmetic  68.6 us (18%)
  starting transfers between devices  35.1 us (9%)
  local copies, waits for them, and re-layouts  19.9 us (5%)
  between operations  14.5 us (4%)
  matrix products  10.5 us (3%)
    all_gather x1, waiting for transfers between devices, per_device(): fetched = lax.all_gather(targets, 'blk', axis=0, tiled=True)  95.9 us
    all_gather x1, blocking collectives, per_device(): near_potential = lax.all_gather(target_potential, 'blk', axis=0, tiled=True)  48.1 us
    all_to_all x2, starting transfers between devices, per_device(): lax.all_to_all(column_peak, 'blk', split_axis=0, concat_axis=0, tiled=True)  25.7 us
    pmax x2, blocking collectives, per_device(): highest = lax.pmax(row_peak, 'rep')  24.8 us
    psum x2, blocking collectives, per_device(): row_total = lax.psum(row_total * jnp.exp(row_peak - highest), 'rep')  21.6 us
    all_to_all x2, waiting for transfers between devices, per_device(): lax.all_to_all(column_total, 'blk', split_axis=0, concat_axis=0, tiled=True)  18.6 us
    reduce_sum x2, other arithmetic, per_device(): jnp.sum(jnp.exp(row_scores - row_tile_max[:, :, None]), axis=2)  17.6 us
    reduce_sum x2, other arithmetic, per_device(): tile_sum = jnp.sum(jnp.exp(scores - tile_max[:, None, :]), axis=1)  17 us
  transfers between devices with their start and end apart: 5, of which 5 were waited for; matrix products, arithmetic and copies ran while one was open for 4% of the time, Pallas kernels for 0%

commit v1 on v0

v1 whole, which is shorter than its diff:
```python
import functools

import jax
import jax.numpy as jnp
from jax import lax
from jax.experimental import pallas as pl
from jax.experimental.pallas import tpu as pltpu
from jax.sharding import Mesh, PartitionSpec as P

epsilon = 0.1
inv_epsilon = 10.0
floor_value = -1e30
sum_low, sum_high = 1e-13, 1e26
pot_low, pot_high = -80.0, 35.0

VM = pl.BlockSpec(memory_space=pltpu.VMEM)
SM = pl.BlockSpec(memory_space=pltpu.SMEM)
ANY = pl.BlockSpec(memory_space=pl.ANY)
MIB = 1024 * 1024

XS, ZS = 4, 8
CHIPS = XS * ZS
DZ = (0, 1, 7, 2, 6, 3, 5, 4)
DX = (0, 1, 3, 2)
GROUPS = ((0, 5), (5, 8))
SLOTS = 2 * CHIPS
CODE, LIST, TROW, SEND, HAS, COUNTS, TABLE = 0, 64, 128, 160, 208, 225, 256


def tile_dot(left, right):
    return lax.dot_general(left, right, (((1,), (1,)), ((), ())), preferred_element_type=jnp.float32)


def all_true(mask):
    return jnp.min(jnp.where(mask, 1.0, 0.0)) > 0.5


def row_to_lanes(row):
    return jnp.broadcast_to(row, (128, 128)).T


def lanes_to_row(tile):
    return jnp.sum(tile.T, axis=0, keepdims=True)


def fold(tile):
    return jnp.sum(tile.reshape(16, 8, tile.shape[1]), axis=0)


def quarters(tile):
    return [tile[:, 128 * q : 128 * (q + 1)] for q in range(4)]


def batched(start, stop, width, wait, body):
    def step(q, _):
        base = start + q * width
        for w in range(width if wait else 0):

            @pl.when(base + w < stop)
            def _():
                wait(base + w)

        for w in range(width):
            body(jnp.minimum(base + w, stop - 1), base + w < stop)
        return 0

    lax.fori_loop(0, (stop - start + width - 1) // width, step, 0)


def pair_of(tab, i):
    slot = tab[LIST + i]
    h = slot & 1
    return slot, h * 8 + (tab[CODE + slot] >> 2), h * CHIPS + tab[TROW + (slot >> 1)]


def table_kernel(named, tab):
    x, z, c = (lax.axis_index(a) for a in ("x", "z", "core"))
    for i in range(HAS, TABLE):
        tab[i] = 0
    count = 0
    for j, dz in enumerate(DZ):
        zt = (z - dz) & (ZS - 1)
        for k, dx in enumerate(DX):
            r = XS * j + k
            row = ((x - dx) & (XS - 1)) * ZS + zt
            tab[TROW + r] = row
            for h in range(2):
                code = named[2 * (x * ZS + z) + (c ^ h), 2 * row + c]
                live = code >= 0
                tab[CODE + 2 * r + h] = code
                tab[LIST + count] = 2 * r + h
                count = count + live.astype(jnp.int32)
                tab[jnp.where(live, HAS + h * 8 + (code >> 2), HAS + 16)] = 1
        for g, (_, end) in enumerate(GROUPS):
            if j + 1 == end:
                tab[COUNTS + 1 + g] = count
        for k, dx in enumerate(DX[1:]):
            far = ((x + dx) & (XS - 1)) * ZS + z
            for h in range(2):
                code = named[2 * far + (c ^ h), 2 * (x * ZS + zt) + c]
                tab[SEND + 16 * k + 2 * j + h] = jnp.where(code >= 0, code & 3, 0)


def stack_kernel(own, sib, both, sem):
    copies = [pltpu.make_async_copy(v, both.at[pl.ds(8 * i, 8)], sem.at[i]) for i, v in enumerate((own, sib))]
    for copy in copies:
        copy.start()
    for copy in copies:
        copy.wait()


def select_kernel(first, n, tab, *refs):
    blocks, outs, sem = refs[:n], refs[n : n + 3], refs[n + 3]
    copies = []
    for k in range(3):
        for j in range(n):
            for h in range(2):
                b = tab[SEND + 16 * k + 2 * (first + j) + h]
                copies.append(
                    pltpu.make_async_copy(blocks[j].at[b], outs[k].at[2 * j + h], sem.at[k, 2 * j + h])
                )
                copies[-1].start()
    for copy in copies:
        copy.wait()


def exact_rows(tab, both, kept, g_ref, total, peak, lse_ref):
    total[...] = jnp.zeros(total.shape, jnp.float32)
    peak[...] = jnp.full(peak.shape, floor_value, jnp.float32)

    def step(i, _):
        slot, s, t = pair_of(tab, i)
        x = tile_dot(kept[slot], both[s])
        if g_ref is not None:
            g = row_to_lanes(g_ref[pl.ds(t, 1), :])
            x = x + jnp.concatenate([g] * 4, axis=1)
        x = x * inv_epsilon
        high = jnp.max(x, axis=0, keepdims=True)
        mass = jnp.sum(jnp.exp(x - high), axis=0, keepdims=True)
        before = peak[pl.ds(s, 1), :]
        raised = jnp.maximum(before, high)
        total[pl.ds(s, 1), :] = total[pl.ds(s, 1), :] * jnp.exp(before - raised) + mass * jnp.exp(high - raised)
        peak[pl.ds(s, 1), :] = raised
        return 0

    lax.fori_loop(0, tab[COUNTS + len(GROUPS)], step, 0)
    for s in range(lse_ref.shape[0]):
        at = pl.ds(s, 1)
        lse_ref[at, :] = jnp.where(tab[HAS + s] > 0, peak[at, :] + jnp.log(total[at, :]), floor_value)


def finish_rows(tab, acc, before, lse_ref):
    ok = jnp.ones((1, lse_ref.shape[1]), jnp.float32)
    for s in range(acc.shape[0]):
        mass = jnp.sum(acc[s], axis=0, keepdims=True)
        if before is not None:
            mass = mass + before[pl.ds(s, 1), :]
        empty = tab[HAS + s] == 0
        fine = empty | ((mass >= sum_low) & (mass <= sum_high))
        ok = jnp.minimum(ok, jnp.where(fine, 1.0, 0.0))
        lse_ref[pl.ds(s, 1), :] = jnp.where(empty, floor_value, jnp.log(mass))
    return jnp.min(ok) > 0.5


def tile_kernel(group, tab, both, *refs):
    first, end = GROUPS[group]
    n, base = end - first, 8 * first
    last = group == len(GROUPS) - 1
    near, far, refs = refs[:n], refs[n : n + 3], refs[n + 3 :]
    if group > 0:
        sums_in, refs = refs[0], refs[3:]
    k_out, kept, sums, acc, t_sem = refs[:5]

    def fetch(slot, block):
        return pltpu.make_async_copy(block, kept.at[slot], t_sem.at[slot - base])

    for j in range(n):
        for k in range(XS):
            for h in range(2):
                local = 8 * j + 2 * k + h
                code = tab[CODE + base + local]

                @pl.when(code >= 0)
                def _():
                    block = near[j].at[code & 3] if k == 0 else far[k - 1].at[2 * j + h]
                    fetch(base + local, block).start()

    acc[...] = jnp.zeros(acc.shape, jnp.float32)

    start, stop = tab[COUNTS + group], tab[COUNTS + group + 1]

    def body(i, live):
        slot, s, _ = pair_of(tab, i)
        k = jnp.exp(tile_dot(kept[slot], both[s]) * inv_epsilon)
        k_out[slot] = k
        acc[s] = acc[s] + fold(k) * live.astype(jnp.float32)

    batched(start, stop, 2, lambda i: fetch(tab[LIST + i], near[0].at[0]).wait(), body)
    if last:
        ok = finish_rows(tab, acc, sums_in, sums)
    else:
        for s in range(acc.shape[0]):
            mass = jnp.sum(acc[s], axis=0, keepdims=True)
            sums[pl.ds(s, 1), :] = mass if group == 0 else mass + sums_in[pl.ds(s, 1), :]

    if last:
        total, peak = refs[5:]

        @pl.when(jnp.logical_not(ok))
        def _():
            exact_rows(tab, both, kept, None, total, peak, sums)


def row_kernel(tab, g_in, k_in, both, kept, lse_ref, gbuf, vbuf, acc, total, peak):
    acc[...] = jnp.zeros(acc.shape, jnp.float32)
    gbuf[pl.ds(0, CHIPS), :] = g_in[:, :128]
    gbuf[pl.ds(CHIPS, CHIPS), :] = g_in[:, 128:]
    scaled = gbuf[...] * inv_epsilon
    vbuf[...] = jnp.exp(scaled)
    fits = all_true((scaled >= pot_low) & (scaled <= pot_high))

    def body(i, live):
        slot, s, t = pair_of(tab, i)
        v = row_to_lanes(vbuf[pl.ds(t, 1), :] * live.astype(jnp.float32))
        part = [fold(k * v) for k in quarters(k_in.at[slot])]
        acc[s] = acc[s] + jnp.concatenate(part, axis=1)

    batched(0, tab[COUNTS + len(GROUPS)], 4, None, body)
    ok = finish_rows(tab, acc, None, lse_ref)

    @pl.when(jnp.logical_not(ok & fits))
    def _():
        exact_rows(tab, both, kept, gbuf, total, peak, lse_ref)


def column_kernel(
    tab, l0, l1, l2, l3, log_a, log_a_sib, k_in, both, kept, f_ref, lse_ref, ubuf, mass, lse
):
    a, b, c, d = l0[...], l1[...], l2[...], l3[...]
    top = jnp.maximum(jnp.maximum(a, c), jnp.maximum(b, d))
    summed = (jnp.exp(a - top) + jnp.exp(c - top)) + (jnp.exp(b - top) + jnp.exp(d - top))
    weights = jnp.concatenate([log_a[...], log_a_sib[...]], axis=0)
    f = epsilon * weights - epsilon * (top + jnp.log(summed))
    f_ref[...] = f[:8]
    scaled = f * inv_epsilon
    fits = all_true((scaled >= pot_low) & (scaled <= pot_high))
    ubuf[...] = jnp.exp(scaled)
    mass[...] = jnp.full(mass.shape, -1.0, jnp.float32)

    def body(i, live):
        slot, s, t = pair_of(tab, i)
        us = quarters(ubuf[pl.ds(s, 1), :])
        ks = quarters(k_in.at[slot])
        part = (ks[0] * us[0] + ks[1] * us[1]) + (ks[2] * us[2] + ks[3] * us[3])
        mass[pl.ds(t, 1), :] = lanes_to_row(part)

    batched(0, tab[COUNTS + len(GROUPS)], 4, None, body)
    m = mass[...]
    dead = m == -1.0
    ok = all_true(dead | ((m >= sum_low) & (m <= sum_high)))
    lse[...] = jnp.where(dead, floor_value, jnp.log(m))

    @pl.when(jnp.logical_not(ok & fits))
    def _():
        ubuf[...] = f

        def exact(i, _):
            slot, s, t = pair_of(tab, i)
            x = (ubuf[pl.ds(s, 1), :] + tile_dot(kept[slot], both[s])) * inv_epsilon
            high = jnp.max(x, axis=1, keepdims=True)
            column = high + jnp.log(jnp.sum(jnp.exp(x - high), axis=1, keepdims=True))
            lse[pl.ds(t, 1), :] = jnp.broadcast_to(column, (128, 128)).T[:1, :]
            return 0

        lax.fori_loop(0, tab[COUNTS + len(GROUPS)], exact, 0)

    lse_ref[:, :128] = lse[pl.ds(0, CHIPS), :]
    lse_ref[:, 128:] = lse[pl.ds(CHIPS, CHIPS), :]


def owner_kernel(parts, wanted, log_b, g_ref, back):
    halves = [parts[:, :128], parts[:, 128:]]
    asked = [jnp.broadcast_to(wanted[:, h : h + 1], halves[h].shape) for h in range(2)]
    outs = [jnp.zeros(halves[h].shape, jnp.float32) for h in range(2)]
    for j in range(g_ref.shape[0]):
        hits = [w == j for w in asked]
        top = functools.reduce(
            jnp.maximum,
            [jnp.max(jnp.where(hit, x, floor_value), axis=0, keepdims=True) for hit, x in zip(hits, halves)],
        )
        mass = sum(
            jnp.sum(jnp.where(hit, jnp.exp(x - top), 0.0), axis=0, keepdims=True) for hit, x in zip(hits, halves)
        )
        g = epsilon * log_b[pl.ds(j, 1), :] - epsilon * (top + jnp.log(mass))
        g_ref[pl.ds(j, 1), :] = g
        outs = [jnp.where(hit, g, out) for hit, out in zip(hits, outs)]
    back[:, :128] = outs[0]
    back[:, 128:] = outs[1]


def shift(value, axis, by):
    n = lax.axis_size(axis)
    return lax.ppermute(value, axis, [(i, (i + by) % n) for i in range(n)])


def per_device(source, targets, log_a, log_b, pair_source, pair_target, pair_count):
    xi, zi, core = (lax.axis_index(a) for a in ("x", "z", "core"))
    local_blocks, quarter, width = targets.shape
    blocks, rows, _ = source.shape
    f32, i32, bf16 = jnp.float32, jnp.int32, jnp.bfloat16
    sds = jax.ShapeDtypeStruct

    def params(mib):
        return pltpu.CompilerParams(vmem_limit_bytes=mib * MIB)

    pin = pltpu.with_memory_space_constraint

    def swap_cores(v):
        return shift(v, "core", 1)

    owners = pair_target.shape[0]
    live = lax.broadcasted_iota(i32, pair_target.shape, 1) < pair_count[:, None]
    match = live[:, None, :] & ((pair_target // local_blocks)[:, None, :] == jnp.arange(owners, dtype=i32)[None, :, None])
    named = jnp.max(jnp.where(match, (pair_source * local_blocks + pair_target % local_blocks)[:, None, :], -1), axis=2)
    tab = pl.pallas_call(table_kernel, out_shape=sds((TABLE,), i32), in_specs=[SM], out_specs=SM)(named)
    tab = pin(tab, pltpu.HBM)
    wanted = lax.dynamic_index_in_dim(named, 2 * (xi * ZS + zi) + core, 1, keepdims=False).reshape(CHIPS, 2)
    wanted = jnp.where(core == 0, wanted, wanted[:, ::-1])
    wanted = jnp.where(wanted >= 0, wanted & 3, -1)

    sib = swap_cores(source)
    log_a_sib = swap_cores(log_a)
    p1, m1 = shift(targets, "z", 1), shift(targets, "z", -1)
    p1, m1, tab = lax.optimization_barrier((p1, m1, tab))
    p2, m2 = shift(p1, "z", 1), shift(m1, "z", -1)
    p3, m3 = shift(p2, "z", 1), shift(m2, "z", -1)
    p4 = shift(p3, "z", 1)
    held = [[pin(v, pltpu.VMEM) for v in group] for group in ((targets, p1, m1, p2, m2), (p3, m3, p4))]

    def along_x(group, after):
        first, end = GROUPS[group]
        n = end - first
        sent = pl.pallas_call(
            functools.partial(select_kernel, first, n),
            out_shape=(pltpu.VMEM((2 * n, quarter, width), bf16),) * 3,
            in_specs=[SM] + [ANY] * n,
            out_specs=(ANY,) * 3,
            scratch_shapes=[pltpu.SemaphoreType.DMA((3, 2 * n))],
            compiler_params=params(4),
        )(tab, *held[group])
        if after is not None:
            held_back = lax.optimization_barrier((*sent, *after))
            sent, after = held_back[:3], held_back[3:]
        return [pin(shift(v, "x", dx), pltpu.VMEM) for v, dx in zip(sent, DX[1:])], after

    tiles = (SLOTS, quarter, rows)
    kept = (SLOTS, quarter, width)
    both = 2 * blocks
    row_scratch = [pltpu.VMEM((both, rows), f32)] * 2
    acc = pltpu.VMEM((both, 8, rows), f32)

    sources = pl.pallas_call(
        stack_kernel,
        out_shape=pltpu.VMEM((both, rows, width), bf16),
        in_specs=[ANY, ANY],
        out_specs=VM,
        scratch_shapes=[pltpu.SemaphoreType.DMA((2,))],
        compiler_params=params(1),
    )(pin(source, pltpu.HBM), sib)

    def tile_call(group, far, before):
        first, end = GROUPS[group]
        slots = 8 * (end - first)
        ins = [tab, pin(sources, pltpu.VMEM), *held[group], *far]
        specs = [SM, VM] + [ANY] * (len(ins) - 2)
        alias = {}
        if before:
            k_tiles, kept_rows, sums = before
            ins += [sums, pin(k_tiles, pltpu.VMEM), pin(kept_rows, pltpu.VMEM)]
            specs += [VM, VM, VM]
            alias = {len(ins) - 2: 0, len(ins) - 1: 1}
        scratch = [acc, pltpu.SemaphoreType.DMA((slots,))]
        if group == len(GROUPS) - 1:
            scratch += row_scratch
        return pl.pallas_call(
            functools.partial(tile_kernel, group),
            out_shape=(pltpu.VMEM(tiles, f32), pltpu.VMEM(kept, bf16), sds((both, rows), f32)),
            in_specs=specs,
            out_specs=(VM, VM, VM),
            scratch_shapes=scratch,
            input_output_aliases=alias,
            compiler_params=params(4),
            cost_estimate=pl.CostEstimate(
                flops=slots * rows * quarter * width, bytes_accessed=10 * MIB, transcendentals=slots * rows * quarter // 2
            ),
        )(*ins)

    near, _ = along_x(0, None)
    far, (wanted, log_a_sib) = along_x(1, (wanted, log_a_sib))
    k_tiles, kept_rows, part = tile_call(1, far, tile_call(0, near, None))

    resident = [pin(v, pltpu.VMEM) for v in (k_tiles, sources, kept_rows)]
    pots = pltpu.VMEM((SLOTS, quarter), f32)
    wide = (CHIPS, 2 * quarter)

    def columns(part):
        other = swap_cores(part)
        other = jnp.concatenate([other[blocks:], other[:blocks]])
        top = jnp.maximum(part, other)
        part = top + jnp.log(jnp.exp(part - top) + jnp.exp(other - top))
        parts = [part] + [shift(part, "rep", k) for k in range(1, 4)]
        return pl.pallas_call(
            column_kernel,
            out_shape=(sds((blocks, rows), f32), sds(wide, f32)),
            in_specs=[SM] + [VM] * 9,
            out_specs=(VM, VM),
            scratch_shapes=[row_scratch[0], pots, pots],
            compiler_params=params(4),
        )(tab, *parts, log_a, log_a_sib, *resident)

    def swap(v):
        return lax.all_to_all(v, ("x", "z"), split_axis=0, concat_axis=0, tiled=True)

    def owner(parts):
        return pl.pallas_call(
            owner_kernel,
            out_shape=(sds((local_blocks, quarter), f32), sds(wide, f32)),
            in_specs=[VM, VM, VM],
            out_specs=(VM, VM),
            compiler_params=params(4),
        )(parts, wanted, log_b)

    f, col = columns(part)
    g, back = owner(swap(col))
    part = pl.pallas_call(
        row_kernel,
        out_shape=sds((both, rows), f32),
        in_specs=[SM] + [VM] * 4,
        out_specs=VM,
        scratch_shapes=[pots, pots, acc, *row_scratch],
        compiler_params=params(4),
    )(tab, swap(back), *resident)
    f, col = columns(part)
    g, _ = owner(swap(col))
    return f, g


def solution(mesh):
    fine = Mesh(mesh.devices.reshape(XS, ZS, 2, 4), ("x", "z", "core", "rep"))
    blk = ("x", "z", "core")
    in_specs = (P(blk, None, None), P(blk, "rep", None), P(blk, None), P(blk, "rep"), P(), P(), P())
    out_specs = (P(blk, None), P(blk, "rep"))
    return jax.shard_map(per_device, mesh=fine, in_specs=in_specs, out_specs=out_specs, check_vma=False)
```

time: 375 us -> 213 us (0.57)
  Pallas kernels: 0 us -> 95.3 us
  waiting for transfers between devices: 131 us -> 36.6 us
  other arithmetic: 68.6 us -> 3.94 us
  blocking collectives: 94.5 us -> 41.3 us
  local copies, waits for them, and re-layouts: 19.9 us -> 2.45 us
  between operations: 14.5 us -> 0.86 us
  matrix products: 10.5 us -> 0 us
    all_gather x1 -> x0, waiting for transfers between devices: 95.9 us -> none  [per_device(): fetched = lax.all_gather(targets, 'blk', axis=0, tiled=True)]
    pallas_call x0 -> x11, Pallas kernels: none -> 95.3 us  [the longest x2 44.4 us: columns(): pl.pallas_call(column_kernel, out_shape=(sds((blocks, rows), f32), sds(wi...]
    all_gather x1 -> x0, blocking collectives: 48.1 us -> none  [per_device(): near_potential = lax.all_gather(target_potential, 'blk', axis=0, tiled=True)]
    all_to_all x0 -> x3, blocking collectives: none -> 41.3 us  [swap(): lax.all_to_all(v, ('x', 'z'), split_axis=0, concat_axis=0, tiled=True)]
    reduce_sum x14 -> x0, other arithmetic: 40.7 us -> none  [the longest x2 17.6 us: per_device(): jnp.sum(jnp.exp(row_scores - row_tile_max[:, :, None]), axis=2)]
    ppermute x0 -> x23, waiting for transfers between devices: none -> 36.6 us  [shift(): return lax.ppermute(value, axis, [(i, (i + by) % n) for i in range(n)])]
    all_to_all x4 -> x0, starting transfers between devices: 35.1 us -> none  [the longest x2 25.7 us: per_device(): lax.all_to_all(column_peak, 'blk', split_axis=0, concat_axis=0, tiled=True)]
    all_to_all x4 -> x0, waiting for transfers between devices: 34.8 us -> none  [the longest x2 18.6 us: per_device(): lax.all_to_all(column_total, 'blk', split_axis=0, concat_axis=0, tiled=True)]
  transfers between devices with their start and end apart: 5 -> 23, of which waited for: 5 -> 14; matrix products, arithmetic and copies ran while one was open for 4% -> 2% of each run, Pallas kernels for 0% -> 7%
where the time goes in v1:
time: 213 us; the launch traced here: 212 us
  Pallas kernels  95.3 us (45%)
  blocking collectives  41.3 us (19%)
  waiting for transfers between devices  36.6 us (17%)
  starting transfers between devices  31.9 us (15%)
  other arithmetic  3.94 us (2%)
  local copies, waits for them, and re-layouts  2.45 us (1%)
    pallas_call x2, Pallas kernels, columns(): pl.pallas_call(column_kernel, out_shape=(sds((blocks, rows), f32), sds(wi...  44.4 us
    all_to_all x3, blocking collectives, swap(): lax.all_to_all(v, ('x', 'z'), split_axis=0, concat_axis=0, tiled=True)  41.3 us
    ppermute x23, waiting for transfers between devices, shift(): return lax.ppermute(value, axis, [(i, (i + by) % n) for i in range(n)])  36.6 us
    ppermute x23, starting transfers between devices, shift(): return lax.ppermute(value, axis, [(i, (i + by) % n) for i in range(n)])  31.9 us
    pallas_call x2, Pallas kernels, tile_call(): pl.pallas_call(functools.partial(tile_kernel, group), out_shape=(pltpu.VM...  25.1 us
    pallas_call x1, Pallas kernels, per_device(): pl.pallas_call(row_kernel, out_shape=sds((both, rows), f32), in_specs=[SM...  15.7 us
    pallas_call x2, Pallas kernels, along_x(): pl.pallas_call(functools.partial(select_kernel, first, n), out_shape=(plt...  4.69 us
  transfers between devices with their start and end apart: 23, of which 14 were waited for; matrix products, arithmetic and copies ran while one was open for 2% of the time, Pallas kernels for 7%

profile of v1, /device:TPU:1, one launch (start us, length us, event | category | flops | bytes accessed | tf_op | source)
XLA Modules:
  0.0 212.3 jit_solution(1278711769494829553)
XLA Ops:
  0.6 3.3 %collective-permute-start.2 = (bf16[8,512,256]{2,1,0:T(8,128)(2,1)}, bf16[8,512,256]{2,1,0:T(8,128)(2,1)S(1)}, u32[]{:S(2)}, u32[]{:S(2)}) collective-permute-start(bf16[8,512,256]{2,1,0:T(8,128)(2,1)} %own.1), channel_id=1, source_target_pairs={{0,4},{4,0},{1,5},{5,1},{2,6},{6,2},{3,7},{7,3},{8,12},{12,8},{9,1... | collective-permute-start | bytes 6291464 | tf_op jit(solution)/shard_map/ppermute | solution.py:303
  4.0 3.9 %collective-permute-start.1 = (bf16[4,128,256]{2,1,0:T(8,128)(2,1)}, bf16[4,128,256]{2,1,0:T(8,128)(2,1)S(1)}, u32[]{:S(2)}, u32[]{:S(2)}) collective-permute-start(bf16[4,128,256]{2,1,0:T(8,128)(2,1)} %refs_0_.3), channel_id=1, source_target_pairs={{0,56},{8,0},{16,8},{24,16},{32,24},{40,32},{48,40},{56,48},{1,57}... | collective-permute-start | bytes 786440 | tf_op jit(solution)/shard_map/ppermute | solution.py:303
  7.8 0.0 collective-permute-start
  7.8 0.8 add_select_fusion.1
  8.6 0.7 iota_compare_fusion.1
  9.3 0.1 copy.20
  9.4 0.1 copy.21
  9.5 2.4 %select_reduce_fusion.named = s32[64,64]{1,0:T(8,128)} fusion(s32[64,48]{1,0:T(8,128)S(1)} %copy.21, s32[64,48]{1,0:T(8,128)S(1)} %copy.20, pred[64,48]{1,0:T(8,128)(4,1)S(1)} %iota_compare_fusion.1), kind=kLoop, calls=%fused_computation | loop fusion | flops 782336 | bytes 44032 | tf_op jit(solution)/shard_map/reduce_max | solution.py:324
  11.8 2.3 %shard_map.86.tab = s32[256]{0:T(256)} custom-call(s32[64,64]{1,0:T(8,128)} %select_reduce_fusion.named), custom_call_target="tpu_custom_call" | custom-call | tf_op jit(solution)/shard_map/pallas_call | solution.py:325
  14.1 2.6 %collective-permute-done.refs_1_ = bf16[4,128,256]{2,1,0:T(8,128)(2,1)S(1)} collective-permute-done((bf16[4,128,256]{2,1,0:T(8,128)(2,1)}, bf16[4,128,256]{2,1,0:T(8,128)(2,1)S(1)}, u32[]{:S(2)}, u32[]{:S(2)}) %collective-permute-start) | collective-permute-done | bytes 262176 | tf_op jit(solution)/shard_map/ppermute | solution.py:303
  16.8 0.0 collective-permute-start.3
  16.8 2.7 %collective-permute-start.5 = (bf16[4,128,256]{2,1,0:T(8,128)(2,1)S(1)}, bf16[4,128,256]{2,1,0:T(8,128)(2,1)S(1)}, u32[]{:S(2)}, u32[]{:S(2)}) collective-permute-start(bf16[4,128,256]{2,1,0:T(8,128)(2,1)S(1)} %collective-permute-done.1.refs_2_), channel_id=1, source_target_pairs={{0,56},{8,0},{16,8},{24,16},{32,24},{40,32},{48,40},{56,48},{1,57}... | collective-permute-start | bytes 786440 | tf_op jit(solution)/shard_map/ppermute | solution.py:303
  19.4 5.1 %collective-permute-done.3.refs_3_ = bf16[4,128,256]{2,1,0:T(8,128)(2,1)S(1)} collective-permute-done((bf16[4,128,256]{2,1,0:T(8,128)(2,1)S(1)}, bf16[4,128,256]{2,1,0:T(8,128)(2,1)S(1)}, u32[]{:S(2)}, u32[]{:S(2)}) %collective-permute-start.3) | collective-permute-done | bytes 262176 | tf_op jit(solution)/shard_map/ppermute | solution.py:303
  24.6 0.0 copy-start
  24.6 1.0 copy-done
  25.7 2.2 %shard_map.89 = (bf16[10,128,256]{2,1,0:T(8,128)(2,1)}, bf16[10,128,256]{2,1,0:T(8,128)(2,1)}, bf16[10,128,256]{2,1,0:T(8,128)(2,1)}) custom-call(s32[256]{0:T(256)} %shard_map.86.tab, bf16[4,128,256]{2,1,0:T(8,128)(2,1)S(1)} %copy-done, bf16[4,128,256]{2,1,0:T(8,128)(2,1)S(1)} %collective-permute-done.refs_1_, ...), custom_call_target="tpu_custom_call" | custom-call | tf_op jit(solution)/shard_map/pallas_call | solution.py:343
  27.9 1.3 collective-permute-start.12
  29.2 2.6 %collective-permute-start.6 = (bf16[4,128,256]{2,1,0:T(8,128)(2,1)S(1)}, bf16[4,128,256]{2,1,0:T(8,128)(2,1)S(1)}, u32[]{:S(2)}, u32[]{:S(2)}) collective-permute-start(bf16[4,128,256]{2,1,0:T(8,128)(2,1)S(1)} %collective-permute-done.5.refs_4_), channel_id=1, source_target_pairs={{0,56},{8,0},{16,8},{24,16},{32,24},{40,32},{48,40},{56,48},{1,57}... | collective-permute-start | bytes 786440 | tf_op jit(solution)/shard_map/ppermute | solution.py:303
  31.8 0.0 collective-permute-done.4.refs_0_
  31.8 0.0 collective-permute-start.7
  31.8 2.2 %collective-permute-start.13 = (bf16[10,128,256]{2,1,0:T(8,128)(2,1)}, bf16[10,128,256]{2,1,0:T(8,128)(2,1)}, u32[]{:S(2)}, u32[]{:S(2)}) collective-permute-start(bf16[10,128,256]{2,1,0:T(8,128)(2,1)} %get-tuple-element.37), channel_id=1, source_target_pairs={{0,192},{64,0},{128,64},{192,128},{1,193},{65,1},{129,65},{193,129... | collective-permute-start | bytes 1966088 | tf_op jit(solution)/shard_map/ppermute | solution.py:303
  34.0 1.1 collective-permute-done.6.refs_1_
  35.1 2.5 %collective-permute-start.14 = (bf16[10,128,256]{2,1,0:T(8,128)(2,1)}, bf16[10,128,256]{2,1,0:T(8,128)(2,1)}, u32[]{:S(2)}, u32[]{:S(2)}) collective-permute-start(bf16[10,128,256]{2,1,0:T(8,128)(2,1)} %get-tuple-element.38), channel_id=1, source_target_pairs={{0,128},{64,192},{128,0},{192,64},{1,129},{65,193},{129,1},{193,65... | collective-permute-start | bytes 1966088 | tf_op jit(solution)/shard_map/ppermute | solution.py:303
  37.5 0.9 dynamic-slice_reduce_fusion
  38.5 0.1 reshape.31
  38.6 0.1 rev.3
  38.7 0.0 collective-permute-done.7.refs_2_
  38.7 3.8 %collective-permute-start.8 = (f32[8,512]{1,0:T(8,128)}, f32[8,512]{1,0:T(8,128)S(1)}, u32[]{:S(2)}, u32[]{:S(2)}) collective-permute-start(f32[8,512]{1,0:T(8,128)} %log_a.3), channel_id=1, source_target_pairs={{0,4},{4,0},{1,5},{5,1},{2,6},{6,2},{3,7},{7,3},{8,12},{12,8},{9,1... | collective-permute-start | bytes 49160 | tf_op jit(solution)/shard_map/ppermute | solution.py:303
  42.5 2.5 %shard_map.88 = (bf16[6,128,256]{2,1,0:T(8,128)(2,1)S(1)}, bf16[6,128,256]{2,1,0:T(8,128)(2,1)S(1)}, bf16[6,128,256]{2,1,0:T(8,128)(2,1)S(1)}) custom-call(s32[256]{0:T(256)} %shard_map.86.tab, bf16[4,128,256]{2,1,0:T(8,128)(2,1)S(1)} %collective-permute-done.4.refs_0_, bf16[4,128,256]{2,1,0:T(8,128)(2,1)S(1)} %collective-permute-done.6.refs_1_, ...), custom_call_target="tpu_custom_call" | custom-call | tf_op jit(solution)/shard_map/pallas_call | solution.py:343
  45.0 0.0 copy-start.1
  45.0 1.1 collective-permute-start.9
  46.1 0.0 collective-permute-done.12.refs_5_
  46.1 1.7 collective-permute-start.10
  47.8 1.2 collective-permute-start.11
  48.9 1.6 shard_map.87.both
  50.5 8.1 %collective-permute-done.14.refs_7_ = bf16[10,128,256]{2,1,0:T(8,128)(2,1)} collective-permute-done((bf16[10,128,256]{2,1,0:T(8,128)(2,1)}, bf16[10,128,256]{2,1,0:T(8,128)(2,1)}, u32[]{:S(2)}, u32[]{:S(2)}) %collective-permute-start.14) | collective-permute-done | bytes 655392 | tf_op jit(solution)/shard_map/ppermute | solution.py:303
  58.7 7.1 %shard_map.90 = (f32[64,128,512]{2,1,0:T(8,128)S(1)}, bf16[64,128,256]{2,1,0:T(8,128)(2,1)S(1)}, f32[16,512]{1,0:T(8,128)S(1)}) custom-call(s32[256]{0:T(256)} %shard_map.86.tab, bf16[16,512,256]{2,1,0:T(8,128)(2,1)S(1)} %shard_map.87.both, bf16[4,128,256]{2,1,0:T(8,128)(2,1)S(1)} %copy-done.1, bf16[4,128,256]{2,1,0:T(8,128)(2,1)S(1)} %collective-permute-done.refs_1_, ...), custom_call_target="tpu_custom_call" | custom-call | flops 671088640 | bytes 10485760 | tf_op jit(solution)/shard_map/pallas_call | solution.py:385
  65.9 5.1 %collective-permute-done.9.refs_3_ = bf16[6,128,256]{2,1,0:T(8,128)(2,1)S(1)} collective-permute-done((bf16[6,128,256]{2,1,0:T(8,128)(2,1)S(1)}, bf16[6,128,256]{2,1,0:T(8,128)(2,1)S(1)}, u32[]{:S(2)}, u32[]{:S(2)}) %collective-permute-start.9) | collective-permute-done | bytes 393248 | tf_op jit(solution)/shard_map/ppermute | solution.py:303
  70.9 4.5 %collective-permute-done.11.refs_5_ = bf16[6,128,256]{2,1,0:T(8,128)(2,1)S(1)} collective-permute-done((bf16[6,128,256]{2,1,0:T(8,128)(2,1)S(1)}, bf16[6,128,256]{2,1,0:T(8,128)(2,1)S(1)}, u32[]{:S(2)}, u32[]{:S(2)}) %collective-permute-start.11) | collective-permute-done | bytes 393248 | tf_op jit(solution)/shard_map/ppermute | solution.py:303
  75.4 18.0 %shard_map.91 = (f32[64,128,512]{2,1,0:T(8,128)S(1)}, bf16[64,128,256]{2,1,0:T(8,128)(2,1)S(1)}, f32[16,512]{1,0:T(8,128)S(1)}) custom-call(s32[256]{0:T(256)} %shard_map.86.tab, bf16[16,512,256]{2,1,0:T(8,128)(2,1)S(1)} %shard_map.87.both, bf16[4,128,256]{2,1,0:T(8,128)(2,1)S(1)} %collective-permute-done.4.refs_0_, ...), custom_call_target="tpu_custom_call", output_to_operand_aliasing={{0}: (9, {}), {1}: (10, {})} | custom-call | flops 402653184 | bytes 10485760 | tf_op jit(solution)/shard_map/pallas_call | solution.py:385
  93.4 2.6 %collective-permute-start.15 = (f32[16,512]{1,0:T(8,128)S(1)}, f32[16,512]{1,0:T(8,128)S(1)}, u32[]{:S(2)}, u32[]{:S(2)}) collective-permute-start(f32[16,512]{1,0:T(8,128)S(1)} %get-tuple-element.42), channel_id=1, source_target_pairs={{0,4},{4,0},{1,5},{5,1},{2,6},{6,2},{3,7},{7,3},{8,12},{12,8},{9,1... | collective-permute-start | bytes 98312 | tf_op jit(solution)/shard_map/ppermute | solution.py:303
  96.0 0.9 collective-permute-done.15
  96.9 0.1 collective-permute-start.18
  97.0 0.1 collective-permute-start.17
  97.1 1.4 collective-permute-start.16
  98.5 1.3 collective-permute-done.18.l3
  99.8 1.6 collective-permute-done.17.l2
  101.4 1.1 collective-permute-done.16.l1
  102.5 22.3 %shard_map.92 = (f32[8,512]{1,0:T(8,128)}, f32[32,256]{1,0:T(8,128)S(1)}) custom-call(s32[256]{0:T(256)} %shard_map.86.tab, f32[16,512]{1,0:T(8,128)S(1)} %log_add_fusion.1.l0, f32[16,512]{1,0:T(8,128)S(1)} %collective-permute-done.16.l1, f32[16,512]{1,0:T(8,128)S(1)} %collective-permute-done.17.l2, f32[16,512]{1,0:T(8,128)S(1)} %collective-permute-done.18.l3, ...), custom_call_target="tpu_custom_call" | custom-call | tf_op jit(solution)/shard_map/pallas_call | solution.py:412
  124.9 15.8 %all_to_all.33 = f32[32,1,256]{2,1,0:T(1,128)S(1)} all-to-all(f32[32,1,256]{2,1,0:T(1,128)S(1)} %copy.22), channel_id=1, replica_groups=mesh['x'=4,'z'=8,'core'=2,'rep'=4] {'x','z'}, dimensions={0} | all-to-all | bytes 65536 | tf_op jit(solution)/shard_map/all_to_all | solution.py:422
  140.6 0.7 shard_map.93
  141.4 11.7 %all_to_all.34 = f32[32,1,256]{2,1,0:T(1,128)S(1)} all-to-all(f32[32,1,256]{2,1,0:T(1,128)S(1)} %copy.23), channel_id=1, replica_groups=mesh['x'=4,'z'=8,'core'=2,'rep'=4] {'x','z'}, dimensions={0} | all-to-all | bytes 65536 | tf_op jit(solution)/shard_map/all_to_all | solution.py:422
  153.1 15.7 %shard_map.94 = f32[16,512]{1,0:T(8,128)S(1)} custom-call(s32[256]{0:T(256)} %shard_map.86.tab, f32[32,256]{1,0:T(8,128)S(1)} %bitcast.12, f32[64,128,512]{2,1,0:T(8,128)S(1)} %get-tuple-element.44.k_in, bf16[16,512,256]{2,1,0:T(8,128)(2,1)S(1)} %shard_map.87.both, bf16[64,128,256]{2,1,0:T(8,128)(2,1)S(1)} %get-tuple-element.45.kept), custom_call_target="tpu_custom_call" | custom-call | tf_op jit(solution)/shard_map/pallas_call | solution.py:435
  168.8 0.1 collective-permute-start.19
  168.9 1.2 collective-permute-done.19
  170.1 0.1 collective-permute-start.22
  170.2 0.1 collective-permute-start.21
  170.3 1.4 collective-permute-start.20
  171.6 1.3 collective-permute-done.22.l3
  172.9 1.6 collective-permute-done.21.l2
  174.5 1.0 collective-permute-done.20.l1
  175.5 22.1 %shard_map.95 = (f32[8,512]{1,0:T(8,128)}, f32[32,256]{1,0:T(8,128)S(1)}) custom-call(s32[256]{0:T(256)} %shard_map.86.tab, f32[16,512]{1,0:T(8,128)S(1)} %log_add_fusion.l0, f32[16,512]{1,0:T(8,128)S(1)} %collective-permute-done.20.l1, f32[16,512]{1,0:T(8,128)S(1)} %collective-permute-done.21.l2, f32[16,512]{1,0:T(8,128)S(1)} %collective-permute-done.22.l3, ...), custom_call_target="tpu_custom_call" | custom-call | tf_op jit(solution)/shard_map/pallas_call | solution.py:412
  197.7 13.9 %all_to_all.35 = f32[32,1,256]{2,1,0:T(1,128)S(1)} all-to-all(f32[32,1,256]{2,1,0:T(1,128)S(1)} %copy.24), channel_id=1, replica_groups=mesh['x'=4,'z'=8,'core'=2,'rep'=4] {'x','z'}, dimensions={0} | all-to-all | bytes 65536 | tf_op jit(solution)/shard_map/all_to_all | solution.py:422
  211.6 0.8 shard_map.96
  (31 shorter events, 0.2 us)
Async XLA Ops:
  0.6 47.1 %collective-permute-start.2 = (bf16[8,512,256]{2,1,0:T(8,128)(2,1)}, bf16[8,512,256]{2,1,0:T(8,128)(2,1)S(1)}, u32[]{:S(2)}, u32[]{:S(2)}) collective-permute-start(bf16[8,512,256]{2,1,0:T(8,128)(2,1)} %own.1), channel_id=1, source_target_pairs={{0,4},{4,0},{1,5},{5,1},{2,6},{6,2},{3,7},{7,3},{8,12},{12,8},{9,1... | collective-permute-start | bytes 6291464 | tf_op jit(solution)/shard_map/ppermute | solution.py:303
  4.0 10.2 %collective-permute-start.1 = (bf16[4,128,256]{2,1,0:T(8,128)(2,1)}, bf16[4,128,256]{2,1,0:T(8,128)(2,1)S(1)}, u32[]{:S(2)}, u32[]{:S(2)}) collective-permute-start(bf16[4,128,256]{2,1,0:T(8,128)(2,1)} %refs_0_.3), channel_id=1, source_target_pairs={{0,56},{8,0},{16,8},{24,16},{32,24},{40,32},{48,40},{56,48},{1,57}... | collective-permute-start | bytes 786440 | tf_op jit(solution)/shard_map/ppermute | solution.py:303
  7.8 9.0 %collective-permute-start = (bf16[4,128,256]{2,1,0:T(8,128)(2,1)}, bf16[4,128,256]{2,1,0:T(8,128)(2,1)S(1)}, u32[]{:S(2)}, u32[]{:S(2)}) collective-permute-start(bf16[4,128,256]{2,1,0:T(8,128)(2,1)} %refs_0_.3), channel_id=1, source_target_pairs={{0,8},{8,16},{16,24},{24,32},{32,40},{40,48},{48,56},{56,0},{1,9},... | collective-permute-start | bytes 786440 | tf_op jit(solution)/shard_map/ppermute | solution.py:303
  16.8 7.8 %collective-permute-start.3 = (bf16[4,128,256]{2,1,0:T(8,128)(2,1)S(1)}, bf16[4,128,256]{2,1,0:T(8,128)(2,1)S(1)}, u32[]{:S(2)}, u32[]{:S(2)}) collective-permute-start(bf16[4,128,256]{2,1,0:T(8,128)(2,1)S(1)} %collective-permute-done.refs_1_), channel_id=1, source_target_pairs={{0,8},{8,16},{16,24},{24,32},{32,40},{40,48},{48,56},{56,0},{1,9},... | collective-permute-start | bytes 786440 | tf_op jit(solution)/shard_map/ppermute | solution.py:303
  16.8 7.8 %collective-permute-start.5 = (bf16[4,128,256]{2,1,0:T(8,128)(2,1)S(1)}, bf16[4,128,256]{2,1,0:T(8,128)(2,1)S(1)}, u32[]{:S(2)}, u32[]{:S(2)}) collective-permute-start(bf16[4,128,256]{2,1,0:T(8,128)(2,1)S(1)} %collective-permute-done.1.refs_2_), channel_id=1, source_target_pairs={{0,56},{8,0},{16,8},{24,16},{32,24},{40,32},{48,40},{56,48},{1,57}... | collective-permute-start | bytes 786440 | tf_op jit(solution)/shard_map/ppermute | solution.py:303
  24.6 7.2 %copy-start.2 = (bf16[4,128,256]{2,1,0:T(8,128)(2,1)}, bf16[4,128,256]{2,1,0:T(8,128)(2,1)S(1)}, u32[]{:S(2)}) copy-start(bf16[4,128,256]{2,1,0:T(8,128)(2,1)S(1)} %collective-permute-done.3.refs_3_) | copy-start | bytes 786436
  24.6 7.2 %collective-permute-start.4 = (bf16[4,128,256]{2,1,0:T(8,128)(2,1)S(1)}, bf16[4,128,256]{2,1,0:T(8,128)(2,1)S(1)}, u32[]{:S(2)}, u32[]{:S(2)}) collective-permute-start(bf16[4,128,256]{2,1,0:T(8,128)(2,1)S(1)} %collective-permute-done.3.refs_3_), channel_id=1, source_target_pairs={{0,8},{8,16},{16,24},{24,32},{32,40},{40,48},{48,56},{56,0},{1,9},... | collective-permute-start | bytes 786440 | tf_op jit(solution)/shard_map/ppermute | solution.py:303
  24.6 1.0 copy-start
  25.7 9.4 %copy-start.4 = (bf16[4,128,256]{2,1,0:T(8,128)(2,1)}, bf16[4,128,256]{2,1,0:T(8,128)(2,1)S(1)}, u32[]{:S(2)}) copy-start(bf16[4,128,256]{2,1,0:T(8,128)(2,1)S(1)} %collective-permute-done.5.refs_4_) | copy-start | bytes 786436
  27.9 18.2 %collective-permute-start.12 = (bf16[10,128,256]{2,1,0:T(8,128)(2,1)}, bf16[10,128,256]{2,1,0:T(8,128)(2,1)}, u32[]{:S(2)}, u32[]{:S(2)}) collective-permute-start(bf16[10,128,256]{2,1,0:T(8,128)(2,1)} %get-tuple-element.36), channel_id=1, source_target_pairs={{0,64},{64,128},{128,192},{192,0},{1,65},{65,129},{129,193},{193,1... | collective-permute-start | bytes 1966088 | tf_op jit(solution)/shard_map/ppermute | solution.py:303
  29.2 5.9 %collective-permute-start.6 = (bf16[4,128,256]{2,1,0:T(8,128)(2,1)S(1)}, bf16[4,128,256]{2,1,0:T(8,128)(2,1)S(1)}, u32[]{:S(2)}, u32[]{:S(2)}) collective-permute-start(bf16[4,128,256]{2,1,0:T(8,128)(2,1)S(1)} %collective-permute-done.5.refs_4_), channel_id=1, source_target_pairs={{0,56},{8,0},{16,8},{24,16},{32,24},{40,32},{48,40},{56,48},{1,57}... | collective-permute-start | bytes 786440 | tf_op jit(solution)/shard_map/ppermute | solution.py:303
  31.8 6.9 %collective-permute-start.7 = (bf16[4,128,256]{2,1,0:T(8,128)(2,1)S(1)}, bf16[4,128,256]{2,1,0:T(8,128)(2,1)S(1)}, u32[]{:S(2)}, u32[]{:S(2)}) collective-permute-start(bf16[4,128,256]{2,1,0:T(8,128)(2,1)S(1)} %collective-permute-done.4.refs_0_), channel_id=1, source_target_pairs={{0,8},{8,16},{16,24},{24,32},{32,40},{40,48},{48,56},{56,0},{1,9},... | collective-permute-start | bytes 786440 | tf_op jit(solution)/shard_map/ppermute | solution.py:303
  31.8 18.8 %collective-permute-start.13 = (bf16[10,128,256]{2,1,0:T(8,128)(2,1)}, bf16[10,128,256]{2,1,0:T(8,128)(2,1)}, u32[]{:S(2)}, u32[]{:S(2)}) collective-permute-start(bf16[10,128,256]{2,1,0:T(8,128)(2,1)} %get-tuple-element.37), channel_id=1, source_target_pairs={{0,192},{64,0},{128,64},{192,128},{1,193},{65,1},{129,65},{193,129... | collective-permute-start | bytes 1966088 | tf_op jit(solution)/shard_map/ppermute | solution.py:303
  35.1 23.6 %collective-permute-start.14 = (bf16[10,128,256]{2,1,0:T(8,128)(2,1)}, bf16[10,128,256]{2,1,0:T(8,128)(2,1)}, u32[]{:S(2)}, u32[]{:S(2)}) collective-permute-start(bf16[10,128,256]{2,1,0:T(8,128)(2,1)} %get-tuple-element.38), channel_id=1, source_target_pairs={{0,128},{64,192},{128,0},{192,64},{1,129},{65,193},{129,1},{193,65... | collective-permute-start | bytes 1966088 | tf_op jit(solution)/shard_map/ppermute | solution.py:303
  38.7 6.3 %collective-permute-start.8 = (f32[8,512]{1,0:T(8,128)}, f32[8,512]{1,0:T(8,128)S(1)}, u32[]{:S(2)}, u32[]{:S(2)}) collective-permute-start(f32[8,512]{1,0:T(8,128)} %log_a.3), channel_id=1, source_target_pairs={{0,4},{4,0},{1,5},{5,1},{2,6},{6,2},{3,7},{7,3},{8,12},{12,8},{9,1... | collective-permute-start | bytes 49160 | tf_op jit(solution)/shard_map/ppermute | solution.py:303
  45.0 13.7 %copy-start.1 = (bf16[4,128,256]{2,1,0:T(8,128)(2,1)S(1)}, bf16[4,128,256]{2,1,0:T(8,128)(2,1)}, u32[]{:S(2)}) copy-start(bf16[4,128,256]{2,1,0:T(8,128)(2,1)} %refs_0_.3) | copy-start | bytes 786436
  45.0 13.7 %copy-start.3 = (bf16[4,128,256]{2,1,0:T(8,128)(2,1)S(1)}, bf16[4,128,256]{2,1,0:T(8,128)(2,1)}, u32[]{:S(2)}) copy-start(bf16[4,128,256]{2,1,0:T(8,128)(2,1)} %copy-done.2) | copy-start | bytes 786436
  45.0 13.7 %copy-start.5 = (bf16[4,128,256]{2,1,0:T(8,128)(2,1)S(1)}, bf16[4,128,256]{2,1,0:T(8,128)(2,1)}, u32[]{:S(2)}) copy-start(bf16[4,128,256]{2,1,0:T(8,128)(2,1)} %copy-done.4) | copy-start | bytes 786436
  45.0 25.9 %collective-permute-start.9 = (bf16[6,128,256]{2,1,0:T(8,128)(2,1)S(1)}, bf16[6,128,256]{2,1,0:T(8,128)(2,1)S(1)}, u32[]{:S(2)}, u32[]{:S(2)}) collective-permute-start(bf16[6,128,256]{2,1,0:T(8,128)(2,1)S(1)} %get-tuple-element.33), channel_id=1, source_target_pairs={{0,64},{64,128},{128,192},{192,0},{1,65},{65,129},{129,193},{193,1... | collective-permute-start | bytes 1179656 | tf_op jit(solution)/shard_map/ppermute | solution.py:303
  46.1 24.8 %collective-permute-start.10 = (bf16[6,128,256]{2,1,0:T(8,128)(2,1)S(1)}, bf16[6,128,256]{2,1,0:T(8,128)(2,1)S(1)}, u32[]{:S(2)}, u32[]{:S(2)}) collective-permute-start(bf16[6,128,256]{2,1,0:T(8,128)(2,1)S(1)} %get-tuple-element.34), channel_id=1, source_target_pairs={{0,192},{64,0},{128,64},{192,128},{1,193},{65,1},{129,65},{193,129... | collective-permute-start | bytes 1179656 | tf_op jit(solution)/shard_map/ppermute | solution.py:303
  47.8 27.7 %collective-permute-start.11 = (bf16[6,128,256]{2,1,0:T(8,128)(2,1)S(1)}, bf16[6,128,256]{2,1,0:T(8,128)(2,1)S(1)}, u32[]{:S(2)}, u32[]{:S(2)}) collective-permute-start(bf16[6,128,256]{2,1,0:T(8,128)(2,1)S(1)} %get-tuple-element.35), channel_id=1, source_target_pairs={{0,128},{64,192},{128,0},{192,64},{1,129},{65,193},{129,1},{193,65... | collective-permute-start | bytes 1179656 | tf_op jit(solution)/shard_map/ppermute | solution.py:303
  75.4 27.1 %copy-start.6 = (f32[8,512]{1,0:T(8,128)S(1)}, f32[8,512]{1,0:T(8,128)}, u32[]{:S(2)}) copy-start(f32[8,512]{1,0:T(8,128)} %log_a.3) | copy-start | bytes 49156
  93.4 3.5 %collective-permute-start.15 = (f32[16,512]{1,0:T(8,128)S(1)}, f32[16,512]{1,0:T(8,128)S(1)}, u32[]{:S(2)}, u32[]{:S(2)}) collective-permute-start(f32[16,512]{1,0:T(8,128)S(1)} %get-tuple-element.42), channel_id=1, source_target_pairs={{0,4},{4,0},{1,5},{5,1},{2,6},{6,2},{3,7},{7,3},{8,12},{12,8},{9,1... | collective-permute-start | bytes 98312 | tf_op jit(solution)/shard_map/ppermute | solution.py:303
  96.9 2.8 %collective-permute-start.18 = (f32[16,512]{1,0:T(8,128)S(1)}, f32[16,512]{1,0:T(8,128)S(1)}, u32[]{:S(2)}, u32[]{:S(2)}) collective-permute-start(f32[16,512]{1,0:T(8,128)S(1)} %log_add_fusion.1.l0), channel_id=1, source_target_pairs={{0,3},{1,0},{2,1},{3,2},{4,7},{5,4},{6,5},{7,6},{8,11},{9,8},{10,9... | collective-permute-start | bytes 98312 | tf_op jit(solution)/shard_map/ppermute | solution.py:303
  97.0 4.4 %collective-permute-start.17 = (f32[16,512]{1,0:T(8,128)S(1)}, f32[16,512]{1,0:T(8,128)S(1)}, u32[]{:S(2)}, u32[]{:S(2)}) collective-permute-start(f32[16,512]{1,0:T(8,128)S(1)} %log_add_fusion.1.l0), channel_id=1, source_target_pairs={{0,2},{1,3},{2,0},{3,1},{4,6},{5,7},{6,4},{7,5},{8,10},{9,11},{10,... | collective-permute-start | bytes 98312 | tf_op jit(solution)/shard_map/ppermute | solution.py:303
  97.1 5.4 %collective-permute-start.16 = (f32[16,512]{1,0:T(8,128)S(1)}, f32[16,512]{1,0:T(8,128)S(1)}, u32[]{:S(2)}, u32[]{:S(2)}) collective-permute-start(f32[16,512]{1,0:T(8,128)S(1)} %log_add_fusion.1.l0), channel_id=1, source_target_pairs={{0,1},{1,2},{2,3},{3,0},{4,5},{5,6},{6,7},{7,4},{8,9},{9,10},{10,1... | collective-permute-start | bytes 98312 | tf_op jit(solution)/shard_map/ppermute | solution.py:303
  102.5 38.1 %copy-start.7 = (f32[4,128]{1,0:T(4,128)S(1)}, f32[4,128]{1,0:T(4,128)}, u32[]{:S(2)}) copy-start(f32[4,128]{1,0:T(4,128)} %log_b.3) | copy-start | bytes 6148
  168.8 1.3 collective-permute-start.19
  170.1 2.8 %collective-permute-start.22 = (f32[16,512]{1,0:T(8,128)S(1)}, f32[16,512]{1,0:T(8,128)S(1)}, u32[]{:S(2)}, u32[]{:S(2)}) collective-permute-start(f32[16,512]{1,0:T(8,128)S(1)} %log_add_fusion.l0), channel_id=1, source_target_pairs={{0,3},{1,0},{2,1},{3,2},{4,7},{5,4},{6,5},{7,6},{8,11},{9,8},{10,9... | collective-permute-start | bytes 98312 | tf_op jit(solution)/shard_map/ppermute | solution.py:303
  170.2 4.4 %collective-permute-start.21 = (f32[16,512]{1,0:T(8,128)S(1)}, f32[16,512]{1,0:T(8,128)S(1)}, u32[]{:S(2)}, u32[]{:S(2)}) collective-permute-start(f32[16,512]{1,0:T(8,128)S(1)} %log_add_fusion.l0), channel_id=1, source_target_pairs={{0,2},{1,3},{2,0},{3,1},{4,6},{5,7},{6,4},{7,5},{8,10},{9,11},{10,... | collective-permute-start | bytes 98312 | tf_op jit(solution)/shard_map/ppermute | solution.py:303
  170.3 5.2 %collective-permute-start.20 = (f32[16,512]{1,0:T(8,128)S(1)}, f32[16,512]{1,0:T(8,128)S(1)}, u32[]{:S(2)}, u32[]{:S(2)}) collective-permute-start(f32[16,512]{1,0:T(8,128)S(1)} %log_add_fusion.l0), channel_id=1, source_target_pairs={{0,1},{1,2},{2,3},{3,0},{4,5},{5,6},{6,7},{7,4},{8,9},{9,10},{10,1... | collective-permute-start | bytes 98312 | tf_op jit(solution)/shard_map/ppermute | solution.py:303

commit v2 on v1

--- a/solution.py
+++ b/solution.py
@@ -22,9 +22,19 @@
 CHIPS = XS * ZS
 DZ = (0, 1, 7, 2, 6, 3, 5, 4)
 DX = (0, 1, 3, 2)
-GROUPS = ((0, 5), (5, 8))
+GROUPS = ((0, 1), (1, 5), (5, 8))
+TILES = ((0, 2), (2, 3))
+
+
+def rows_of(group, k):
+    if k == XS - 1 and group < 2:
+        return ((0, 0), (0, GROUPS[1][1]))[group]
+    return GROUPS[group]
+
+
+PARTS = [(g, k) for g in range(len(GROUPS)) for k in range(XS) if rows_of(g, k)[0] < rows_of(g, k)[1]]
 SLOTS = 2 * CHIPS
-CODE, LIST, TROW, SEND, HAS, COUNTS, TABLE = 0, 64, 128, 160, 208, 225, 256
+CODE, LIST, TROW, SEND, HAS, COUNTS, TABLE = 0, 64, 128, 160, 224, 241, 256
 
 
 def tile_dot(left, right):
@@ -91,10 +101,10 @@
                 tab[LIST + count] = 2 * r + h
                 count = count + live.astype(jnp.int32)
                 tab[jnp.where(live, HAS + h * 8 + (code >> 2), HAS + 16)] = 1
-        for g, (_, end) in enumerate(GROUPS):
-            if j + 1 == end:
+        for g, (_, end) in enumerate(TILES):
+            if j + 1 == GROUPS[end - 1][1]:
                 tab[COUNTS + 1 + g] = count
-        for k, dx in enumerate(DX[1:]):
+        for k, dx in enumerate(DX):
             far = ((x + dx) & (XS - 1)) * ZS + z
             for h in range(2):
                 code = named[2 * far + (c ^ h), 2 * (x * ZS + zt) + c]
@@ -109,16 +119,17 @@
         copy.wait()
 
 
-def select_kernel(first, n, tab, *refs):
-    blocks, outs, sem = refs[:n], refs[n : n + 3], refs[n + 3]
+def select_kernel(group, n, tab, *refs):
+    blocks, outs, sem = refs[:n], refs[n:-1], refs[-1]
+    base = GROUPS[group][1] - n
     copies = []
-    for k in range(3):
-        for j in range(n):
+    for out, k in zip(outs, [k for g, k in PARTS if g == group]):
+        low, high = rows_of(group, k)
+        for j in range(low, high):
             for h in range(2):
-                b = tab[SEND + 16 * k + 2 * (first + j) + h]
-                copies.append(
-                    pltpu.make_async_copy(blocks[j].at[b], outs[k].at[2 * j + h], sem.at[k, 2 * j + h])
-                )
+                i = 2 * (j - low) + h
+                b = tab[SEND + 16 * k + 2 * j + h]
+                copies.append(pltpu.make_async_copy(blocks[j - base].at[b], out.at[i], sem.at[k, i]))
                 copies[-1].start()
     for copy in copies:
         copy.wait()
@@ -143,7 +154,7 @@
         peak[pl.ds(s, 1), :] = raised
         return 0
 
-    lax.fori_loop(0, tab[COUNTS + len(GROUPS)], step, 0)
+    lax.fori_loop(0, tab[COUNTS + len(TILES)], step, 0)
     for s in range(lse_ref.shape[0]):
         at = pl.ds(s, 1)
         lse_ref[at, :] = jnp.where(tab[HAS + s] > 0, peak[at, :] + jnp.log(total[at, :]), floor_value)
@@ -163,10 +174,12 @@
 
 
 def tile_kernel(group, tab, both, *refs):
-    first, end = GROUPS[group]
+    groups = GROUPS[slice(*TILES[group])]
+    first, end = groups[0][0], groups[-1][1]
     n, base = end - first, 8 * first
-    last = group == len(GROUPS) - 1
-    near, far, refs = refs[:n], refs[n : n + 3], refs[n + 3 :]
+    last = group == len(TILES) - 1
+    here = [(g, k) for g, k in PARTS if GROUPS[g] in groups]
+    parts, refs = refs[: len(here)], refs[len(here) :]
     if group > 0:
         sums_in, refs = refs[0], refs[3:]
     k_out, kept, sums, acc, t_sem = refs[:5]
@@ -174,16 +187,15 @@
     def fetch(slot, block):
         return pltpu.make_async_copy(block, kept.at[slot], t_sem.at[slot - base])
 
-    for j in range(n):
-        for k in range(XS):
+    for part, (g, k) in zip(parts, here):
+        low, high = rows_of(g, k)
+        for j in range(low, high):
             for h in range(2):
-                local = 8 * j + 2 * k + h
-                code = tab[CODE + base + local]
-
-                @pl.when(code >= 0)
+                slot = 8 * j + 2 * k + h
+
+                @pl.when(tab[CODE + slot] >= 0)
                 def _():
-                    block = near[j].at[code & 3] if k == 0 else far[k - 1].at[2 * j + h]
-                    fetch(base + local, block).start()
+                    fetch(slot, part.at[2 * (j - low) + h]).start()
 
     acc[...] = jnp.zeros(acc.shape, jnp.float32)
 
@@ -195,7 +207,7 @@
         k_out[slot] = k
         acc[s] = acc[s] + fold(k) * live.astype(jnp.float32)
 
-    batched(start, stop, 2, lambda i: fetch(tab[LIST + i], near[0].at[0]).wait(), body)
+    batched(start, stop, 2, lambda i: fetch(tab[LIST + i], parts[0].at[0]).wait(), body)
     if last:
         ok = finish_rows(tab, acc, sums_in, sums)
     else:
@@ -225,7 +237,7 @@
         part = [fold(k * v) for k in quarters(k_in.at[slot])]
         acc[s] = acc[s] + jnp.concatenate(part, axis=1)
 
-    batched(0, tab[COUNTS + len(GROUPS)], 4, None, body)
+    batched(0, tab[COUNTS + len(TILES)], 4, None, body)
     ok = finish_rows(tab, acc, None, lse_ref)
 
     @pl.when(jnp.logical_not(ok & fits))
@@ -254,7 +266,7 @@
         part = (ks[0] * us[0] + ks[1] * us[1]) + (ks[2] * us[2] + ks[3] * us[3])
         mass[pl.ds(t, 1), :] = lanes_to_row(part)
 
-    batched(0, tab[COUNTS + len(GROUPS)], 4, None, body)
+    batched(0, tab[COUNTS + len(TILES)], 4, None, body)
     m = mass[...]
     dead = m == -1.0
     ok = all_true(dead | ((m >= sum_low) & (m <= sum_high)))
@@ -272,7 +284,7 @@
             lse[pl.ds(t, 1), :] = jnp.broadcast_to(column, (128, 128)).T[:1, :]
             return 0
 
-        lax.fori_loop(0, tab[COUNTS + len(GROUPS)], exact, 0)
+        lax.fori_loop(0, tab[COUNTS + len(TILES)], exact, 0)
 
     lse_ref[:, :128] = lse[pl.ds(0, CHIPS), :]
     lse_ref[:, 128:] = lse[pl.ds(CHIPS, CHIPS), :]
@@ -333,25 +345,30 @@
     p1, m1 = shift(targets, "z", 1), shift(targets, "z", -1)
     p1, m1, tab = lax.optimization_barrier((p1, m1, tab))
     p2, m2 = shift(p1, "z", 1), shift(m1, "z", -1)
+
+    def select(group, *blocks):
+        n = len(blocks)
+        spans = [rows_of(group, k) for g, k in PARTS if g == group]
+        return pl.pallas_call(
+            functools.partial(select_kernel, group, n),
+            out_shape=[pltpu.VMEM((2 * (high - low), quarter, width), bf16) for low, high in spans],
+            in_specs=[SM] + [ANY] * n,
+            out_specs=[ANY] * len(spans),
+            scratch_shapes=[pltpu.SemaphoreType.DMA((XS, 10))],
+            compiler_params=params(4),
+        )(tab, *[pin(v, pltpu.VMEM) for v in blocks])
+
+    def along_x(blocks):
+        return [blocks[0], *[shift(v, "x", dx) for v, dx in zip(blocks[1:], DX[1:])]]
+
+    first = along_x(select(0, targets))
     p3, m3 = shift(p2, "z", 1), shift(m2, "z", -1)
     p4 = shift(p3, "z", 1)
-    held = [[pin(v, pltpu.VMEM) for v in group] for group in ((targets, p1, m1, p2, m2), (p3, m3, p4))]
-
-    def along_x(group, after):
-        first, end = GROUPS[group]
-        n = end - first
-        sent = pl.pallas_call(
-            functools.partial(select_kernel, first, n),
-            out_shape=(pltpu.VMEM((2 * n, quarter, width), bf16),) * 3,
-            in_specs=[SM] + [ANY] * n,
-            out_specs=(ANY,) * 3,
-            scratch_shapes=[pltpu.SemaphoreType.DMA((3, 2 * n))],
-            compiler_params=params(4),
-        )(tab, *held[group])
-        if after is not None:
-            held_back = lax.optimization_barrier((*sent, *after))
-            sent, after = held_back[:3], held_back[3:]
-        return [pin(shift(v, "x", dx), pltpu.VMEM) for v, dx in zip(sent, DX[1:])], after
+    second = select(1, targets, p1, m1, p2, m2)
+    second, first = lax.optimization_barrier((second, first))
+    second = along_x(second)
+    third = along_x(select(2, p3, m3, p4))
+    held = [first, *[[pin(v, pltpu.VMEM) for v in group] for group in (second, third)]]
 
     tiles = (SLOTS, quarter, rows)
     kept = (SLOTS, quarter, width)
@@ -368,10 +385,11 @@
         compiler_params=params(1),
     )(pin(source, pltpu.HBM), sib)
 
-    def tile_call(group, far, before):
-        first, end = GROUPS[group]
+    def tile_call(group, before):
+        groups = slice(*TILES[group])
+        first, end = GROUPS[groups][0][0], GROUPS[groups][-1][1]
         slots = 8 * (end - first)
-        ins = [tab, pin(sources, pltpu.VMEM), *held[group], *far]
+        ins = [tab, pin(sources, pltpu.VMEM), *sum(held[groups], [])]
         specs = [SM, VM] + [ANY] * (len(ins) - 2)
         alias = {}
         if before:
@@ -380,7 +398,7 @@
             specs += [VM, VM, VM]
             alias = {len(ins) - 2: 0, len(ins) - 1: 1}
         scratch = [acc, pltpu.SemaphoreType.DMA((slots,))]
-        if group == len(GROUPS) - 1:
+        if group == len(TILES) - 1:
             scratch += row_scratch
         return pl.pallas_call(
             functools.partial(tile_kernel, group),
@@ -395,9 +413,9 @@
             ),
         )(*ins)
 
-    near, _ = along_x(0, None)
-    far, (wanted, log_a_sib) = along_x(1, (wanted, log_a_sib))
-    k_tiles, kept_rows, part = tile_call(1, far, tile_call(0, near, None))
+    k_tiles, kept_rows, sums = tile_call(0, None)
+    sums, wanted, log_a_sib = lax.optimization_barrier((sums, wanted, log_a_sib))
+    k_tiles, kept_rows, part = tile_call(1, (k_tiles, kept_rows, sums))
 
     resident = [pin(v, pltpu.VMEM) for v in (k_tiles, sources, kept_rows)]
     pots = pltpu.VMEM((SLOTS, quarter), f32)

time: 213 us -> 208 us (0.977)
  waiting for transfers between devices: 36.6 us -> 24.2 us
  Pallas kernels: 95.3 us -> 83.2 us
  starting transfers between devices: 31.9 us -> 41 us
  blocking collectives: 41.3 us -> 46.4 us
  local copies, waits for them, and re-layouts: 2.45 us -> 6.33 us
    ppermute x23 -> x25, waiting for transfers between devices: 36.6 us -> 24.2 us  [shift(): return lax.ppermute(value, axis, [(i, (i + by) % n) for i in range(n)])]
    ppermute x23 -> x25, starting transfers between devices: 31.9 us -> 41 us  [shift(): return lax.ppermute(value, axis, [(i, (i + by) % n) for i in range(n)])]
    pallas_call x2, Pallas kernels: 44.4 us -> 36 us  [columns(): pl.pallas_call(column_kernel, out_shape=(sds((blocks, rows), f32), sds(wi...]
    all_to_all x3, blocking collectives: 41.3 us -> 46.4 us  [swap(): lax.all_to_all(v, ('x', 'z'), split_axis=0, concat_axis=0, tiled=True)]
    pallas_call x2, Pallas kernels: 25.1 us -> 21.5 us  [tile_call(): pl.pallas_call(functools.partial(tile_kernel, group), out_shape=(pltpu.VM...]
    pallas_call x1, Pallas kernels: 15.7 us -> 12.7 us  [per_device(): pl.pallas_call(row_kernel, out_shape=sds((both, rows), f32), in_specs=[SM...]
    pallas_call x2 -> x3, Pallas kernels: 4.69 us -> 7.68 us  [select(): pl.pallas_call(functools.partial(select_kernel, group, n), out_shape=[plt...]
  transfers between devices with their start and end apart: 23 -> 25, of which waited for: 14 -> 13; matrix products, arithmetic and copies ran while one was open for 2% -> 4% of each run, Pallas kernels for 7% -> 9%
where the time goes in v2:
time: 208 us; the launch traced here: 207 us
  Pallas kernels  83.2 us (40%)
  blocking collectives  46.4 us (22%)
  starting transfers between devices  41 us (20%)
  waiting for transfers between devices  24.2 us (12%)
  local copies, waits for them, and re-layouts  6.33 us (3%)
  other arithmetic  4.67 us (2%)
    all_to_all x3, blocking collectives, swap(): lax.all_to_all(v, ('x', 'z'), split_axis=0, concat_axis=0, tiled=True)  46.4 us
    ppermute x25, starting transfers between devices, shift(): return lax.ppermute(value, axis, [(i, (i + by) % n) for i in range(n)])  41 us
    pallas_call x2, Pallas kernels, columns(): pl.pallas_call(column_kernel, out_shape=(sds((blocks, rows), f32), sds(wi...  36 us
    ppermute x25, waiting for transfers between devices, shift(): return lax.ppermute(value, axis, [(i, (i + by) % n) for i in range(n)])  24.2 us
    pallas_call x2, Pallas kernels, tile_call(): pl.pallas_call(functools.partial(tile_kernel, group), out_shape=(pltpu.VM...  21.5 us
    pallas_call x1, Pallas kernels, per_device(): pl.pallas_call(row_kernel, out_shape=sds((both, rows), f32), in_specs=[SM...  12.7 us
    pallas_call x3, Pallas kernels, select(): pl.pallas_call(functools.partial(select_kernel, group, n), out_shape=[plt...  7.68 us
  transfers between devices with their start and end apart: 25, of which 13 were waited for; matrix products, arithmetic and copies ran while one was open for 4% of the time, Pallas kernels for 9%

profile of v2, /device:TPU:1, one launch (start us, length us, event | category | flops | bytes accessed | tf_op | source)
XLA Modules:
  0.0 206.8 jit_solution(11258990788824955089)
XLA Ops:
  0.6 3.3 %collective-permute-start.2 = (bf16[8,512,256]{2,1,0:T(8,128)(2,1)}, bf16[8,512,256]{2,1,0:T(8,128)(2,1)S(1)}, u32[]{:S(2)}, u32[]{:S(2)}) collective-permute-start(bf16[8,512,256]{2,1,0:T(8,128)(2,1)} %own.1), channel_id=1, source_target_pairs={{0,4},{4,0},{1,5},{5,1},{2,6},{6,2},{3,7},{7,3},{8,12},{12,8},{9,1... | collective-permute-start | bytes 6291464 | tf_op jit(solution)/shard_map/ppermute | solution.py:315
  4.0 3.9 %collective-permute-start.1 = (bf16[4,128,256]{2,1,0:T(8,128)(2,1)}, bf16[4,128,256]{2,1,0:T(8,128)(2,1)S(1)}, u32[]{:S(2)}, u32[]{:S(2)}) collective-permute-start(bf16[4,128,256]{2,1,0:T(8,128)(2,1)} %refs_0_.3), channel_id=1, source_target_pairs={{0,56},{8,0},{16,8},{24,16},{32,24},{40,32},{48,40},{56,48},{1,57}... | collective-permute-start | bytes 786440 | tf_op jit(solution)/shard_map/ppermute | solution.py:315
  7.8 0.8 add_select_fusion.1
  8.6 0.7 iota_compare_fusion.1
  9.3 0.1 copy.20
  9.4 0.1 copy.21
  9.5 2.4 %select_reduce_fusion.named = s32[64,64]{1,0:T(8,128)} fusion(s32[64,48]{1,0:T(8,128)S(1)} %copy.21, s32[64,48]{1,0:T(8,128)S(1)} %copy.20, pred[64,48]{1,0:T(8,128)(4,1)S(1)} %iota_compare_fusion.1), kind=kLoop, calls=%fused_computation | loop fusion | flops 782336 | bytes 44032 | tf_op jit(solution)/shard_map/reduce_max | solution.py:336
  11.9 2.3 %shard_map.86.tab = s32[256]{0:T(256)} custom-call(s32[64,64]{1,0:T(8,128)} %select_reduce_fusion.named), custom_call_target="tpu_custom_call" | custom-call | tf_op jit(solution)/shard_map/pallas_call | solution.py:337
  14.2 0.0 collective-permute-done.1.refs_2_
  14.2 2.6 %collective-permute-done.refs_1_ = bf16[4,128,256]{2,1,0:T(8,128)(2,1)S(1)} collective-permute-done((bf16[4,128,256]{2,1,0:T(8,128)(2,1)}, bf16[4,128,256]{2,1,0:T(8,128)(2,1)S(1)}, u32[]{:S(2)}, u32[]{:S(2)}) %collective-permute-start) | collective-permute-done | bytes 262176 | tf_op jit(solution)/shard_map/ppermute | solution.py:315
  16.8 0.0 collective-permute-start.3
  16.8 2.7 %collective-permute-start.5 = (bf16[4,128,256]{2,1,0:T(8,128)(2,1)S(1)}, bf16[4,128,256]{2,1,0:T(8,128)(2,1)S(1)}, u32[]{:S(2)}, u32[]{:S(2)}) collective-permute-start(bf16[4,128,256]{2,1,0:T(8,128)(2,1)S(1)} %collective-permute-done.1.refs_2_), channel_id=1, source_target_pairs={{0,56},{8,0},{16,8},{24,16},{32,24},{40,32},{48,40},{56,48},{1,57}... | collective-permute-start | bytes 786440 | tf_op jit(solution)/shard_map/ppermute | solution.py:315
  19.4 0.9 copy-done
  20.4 1.6 shard_map.90
  22.0 1.3 collective-permute-start.11
  23.3 1.5 collective-permute-start.12
  24.7 0.0 collective-permute-done.3.refs_3_
  24.8 3.5 %shard_map.89 = (bf16[8,128,256]{2,1,0:T(8,128)(2,1)S(1)}, bf16[8,128,256]{2,1,0:T(8,128)(2,1)S(1)}, bf16[8,128,256]{2,1,0:T(8,128)(2,1)}, bf16[10,128,256]{2,1,0:T(8,128)(2,1)}) custom-call(s32[256]{0:T(256)} %shard_map.86.tab, bf16[4,128,256]{2,1,0:T(8,128)(2,1)S(1)} %copy-done, bf16[4,128,256]{2,1,0:T(8,128)(2,1)S(1)} %collective-permute-done.refs_1_, ...), custom_call_target="tpu_custom_call" | custom-call | tf_op jit(solution)/shard_map/pallas_call | solution.py:352
  28.3 0.0 collective-permute-done.12.refs_2_
  28.3 0.6 copy-done.5
  28.9 1.1 collective-permute-start.13
  30.0 2.7 %collective-permute-start.6 = (bf16[4,128,256]{2,1,0:T(8,128)(2,1)S(1)}, bf16[4,128,256]{2,1,0:T(8,128)(2,1)S(1)}, u32[]{:S(2)}, u32[]{:S(2)}) collective-permute-start(bf16[4,128,256]{2,1,0:T(8,128)(2,1)S(1)} %collective-permute-done.5.refs_4_), channel_id=1, source_target_pairs={{0,56},{8,0},{16,8},{24,16},{32,24},{40,32},{48,40},{56,48},{1,57}... | collective-permute-start | bytes 786440 | tf_op jit(solution)/shard_map/ppermute | solution.py:315
  32.7 2.5 %collective-permute-start.15 = (bf16[10,128,256]{2,1,0:T(8,128)(2,1)}, bf16[10,128,256]{2,1,0:T(8,128)(2,1)S(1)}, u32[]{:S(2)}, u32[]{:S(2)}) collective-permute-start(bf16[10,128,256]{2,1,0:T(8,128)(2,1)} %get-tuple-element.57), channel_id=1, source_target_pairs={{0,128},{64,192},{128,0},{192,64},{1,129},{65,193},{129,1},{193,65... | collective-permute-start | bytes 1966088 | tf_op jit(solution)/shard_map/ppermute | solution.py:315
  35.1 0.9 collective-permute-done.6.refs_1_
  36.0 1.6 collective-permute-start.14
  37.6 4.3 %collective-permute-done.7.refs_2_ = bf16[4,128,256]{2,1,0:T(8,128)(2,1)S(1)} collective-permute-done((bf16[4,128,256]{2,1,0:T(8,128)(2,1)S(1)}, bf16[4,128,256]{2,1,0:T(8,128)(2,1)S(1)}, u32[]{:S(2)}, u32[]{:S(2)}) %collective-permute-start.7) | collective-permute-done | bytes 262176 | tf_op jit(solution)/shard_map/ppermute | solution.py:315
  41.8 2.6 %shard_map.88 = (bf16[6,128,256]{2,1,0:T(8,128)(2,1)S(1)}, bf16[6,128,256]{2,1,0:T(8,128)(2,1)}, bf16[6,128,256]{2,1,0:T(8,128)(2,1)}, bf16[6,128,256]{2,1,0:T(8,128)(2,1)}) custom-call(s32[256]{0:T(256)} %shard_map.86.tab, bf16[4,128,256]{2,1,0:T(8,128)(2,1)S(1)} %collective-permute-done.4.refs_0_, bf16[4,128,256]{2,1,0:T(8,128)(2,1)S(1)} %collective-permute-done.6.refs_1_, ...), custom_call_target="tpu_custom_call" | custom-call | tf_op jit(solution)/shard_map/pallas_call | solution.py:352
  44.5 0.7 copy-done.3
  45.2 0.8 copy-done.1
  46.0 2.7 %collective-permute-start.9 = (bf16[6,128,256]{2,1,0:T(8,128)(2,1)}, bf16[6,128,256]{2,1,0:T(8,128)(2,1)}, u32[]{:S(2)}, u32[]{:S(2)}) collective-permute-start(bf16[6,128,256]{2,1,0:T(8,128)(2,1)} %get-tuple-element.42), channel_id=1, source_target_pairs={{0,192},{64,0},{128,64},{192,128},{1,193},{65,1},{129,65},{193,129... | collective-permute-start | bytes 1179656 | tf_op jit(solution)/shard_map/ppermute | solution.py:315
  48.7 1.5 dynamic-slice_reduce_fusion
  50.2 0.7 reshape.31
  50.9 0.7 rev.3
  51.6 0.7 and_select_fusion.wanted
  52.3 1.7 shard_map.87.both
  54.0 6.5 %collective-permute-done.14.refs_5_ = bf16[8,128,256]{2,1,0:T(8,128)(2,1)} collective-permute-done((bf16[8,128,256]{2,1,0:T(8,128)(2,1)}, bf16[8,128,256]{2,1,0:T(8,128)(2,1)}, u32[]{:S(2)}, u32[]{:S(2)}) %collective-permute-start.14) | collective-permute-done | bytes 524320 | tf_op jit(solution)/shard_map/ppermute | solution.py:315
  60.6 5.2 %collective-permute-start.16 = (f32[8,512]{1,0:T(8,128)S(1)}, f32[8,512]{1,0:T(8,128)S(1)}, u32[]{:S(2)}, u32[]{:S(2)}) collective-permute-start(f32[8,512]{1,0:T(8,128)S(1)} %copy-done.7), channel_id=1, source_target_pairs={{0,4},{4,0},{1,5},{5,1},{2,6},{6,2},{3,7},{7,3},{8,12},{12,8},{9,1... | collective-permute-start | bytes 49160 | tf_op jit(solution)/shard_map/ppermute | solution.py:315
  65.8 7.1 %shard_map.91 = (f32[64,128,512]{2,1,0:T(8,128)S(1)}, bf16[64,128,256]{2,1,0:T(8,128)(2,1)S(1)}, f32[16,512]{1,0:T(8,128)S(1)}) custom-call(s32[256]{0:T(256)} %shard_map.86.tab, bf16[16,512,256]{2,1,0:T(8,128)(2,1)S(1)} %shard_map.87.both, bf16[2,128,256]{2,1,0:T(8,128)(2,1)S(1)} %get-tuple-element.51.refs_0_, ...), custom_call_target="tpu_custom_call" | custom-call | flops 671088640 | bytes 10485760 | tf_op jit(solution)/shard_map/pallas_call | solution.py:403
  72.9 0.2 collective-permute-done.10.refs_3_
  73.1 14.4 %shard_map.92 = (f32[64,128,512]{2,1,0:T(8,128)S(1)}, bf16[64,128,256]{2,1,0:T(8,128)(2,1)S(1)}, f32[16,512]{1,0:T(8,128)S(1)}) custom-call(s32[256]{0:T(256)} %shard_map.86.tab, bf16[16,512,256]{2,1,0:T(8,128)(2,1)S(1)} %shard_map.87.both, bf16[6,128,256]{2,1,0:T(8,128)(2,1)S(1)} %copy-done.4, ...), custom_call_target="tpu_custom_call", output_to_operand_aliasing={{0}: (7, {}), {1}: (8, {})} | custom-call | flops 402653184 | bytes 10485760 | tf_op jit(solution)/shard_map/pallas_call | solution.py:403
  87.5 2.0 collective-permute-start.17
  89.5 0.9 collective-permute-done.17
  90.4 0.1 collective-permute-start.20
  90.5 0.1 collective-permute-start.19
  90.6 1.4 collective-permute-start.18
  91.9 1.3 collective-permute-done.20.l3
  93.2 1.6 collective-permute-done.19.l2
  94.8 1.1 collective-permute-done.18.l1
  96.0 18.1 %shard_map.93 = (f32[8,512]{1,0:T(8,128)}, f32[32,256]{1,0:T(8,128)S(1)}) custom-call(s32[256]{0:T(256)} %shard_map.86.tab, f32[16,512]{1,0:T(8,128)S(1)} %log_add_fusion.1.l0, f32[16,512]{1,0:T(8,128)S(1)} %collective-permute-done.18.l1, f32[16,512]{1,0:T(8,128)S(1)} %collective-permute-done.19.l2, f32[16,512]{1,0:T(8,128)S(1)} %collective-permute-done.20.l3, ...), custom_call_target="tpu_custom_call" | custom-call | tf_op jit(solution)/shard_map/pallas_call | solution.py:430
  114.1 19.2 %all_to_all.33 = f32[32,1,256]{2,1,0:T(1,128)S(1)} all-to-all(f32[32,1,256]{2,1,0:T(1,128)S(1)} %copy.22), channel_id=1, replica_groups=mesh['x'=4,'z'=8,'core'=2,'rep'=4] {'x','z'}, dimensions={0} | all-to-all | bytes 65536 | tf_op jit(solution)/shard_map/all_to_all | solution.py:440
  133.3 0.7 shard_map.94
  134.1 11.7 %all_to_all.34 = f32[32,1,256]{2,1,0:T(1,128)S(1)} all-to-all(f32[32,1,256]{2,1,0:T(1,128)S(1)} %copy.23), channel_id=1, replica_groups=mesh['x'=4,'z'=8,'core'=2,'rep'=4] {'x','z'}, dimensions={0} | all-to-all | bytes 65536 | tf_op jit(solution)/shard_map/all_to_all | solution.py:440
  145.7 12.7 %shard_map.95 = f32[16,512]{1,0:T(8,128)S(1)} custom-call(s32[256]{0:T(256)} %shard_map.86.tab, f32[32,256]{1,0:T(8,128)S(1)} %bitcast.12, f32[64,128,512]{2,1,0:T(8,128)S(1)} %get-tuple-element.64.k_in, bf16[16,512,256]{2,1,0:T(8,128)(2,1)S(1)} %shard_map.87.both, bf16[64,128,256]{2,1,0:T(8,128)(2,1)S(1)} %get-tuple-element.65.kept), custom_call_target="tpu_custom_call" | custom-call | tf_op jit(solution)/shard_map/pallas_call | solution.py:453
  158.4 7.7 %collective-permute-start.21 = (f32[16,512]{1,0:T(8,128)S(1)}, f32[16,512]{1,0:T(8,128)S(1)}, u32[]{:S(2)}, u32[]{:S(2)}) collective-permute-start(f32[16,512]{1,0:T(8,128)S(1)} %shard_map.95), channel_id=1, source_target_pairs={{0,4},{4,0},{1,5},{5,1},{2,6},{6,2},{3,7},{7,3},{8,12},{12,8},{9,1... | collective-permute-start | bytes 98312 | tf_op jit(solution)/shard_map/ppermute | solution.py:315
  166.1 0.9 collective-permute-done.21
  167.0 0.1 collective-permute-start.24
  167.1 0.1 collective-permute-start.23
  167.2 1.4 collective-permute-start.22
  168.5 1.3 collective-permute-done.24.l3
  169.8 1.6 collective-permute-done.23.l2
  171.4 1.1 collective-permute-done.22.l1
  172.6 17.9 %shard_map.96 = (f32[8,512]{1,0:T(8,128)}, f32[32,256]{1,0:T(8,128)S(1)}) custom-call(s32[256]{0:T(256)} %shard_map.86.tab, f32[16,512]{1,0:T(8,128)S(1)} %log_add_fusion.l0, f32[16,512]{1,0:T(8,128)S(1)} %collective-permute-done.22.l1, f32[16,512]{1,0:T(8,128)S(1)} %collective-permute-done.23.l2, f32[16,512]{1,0:T(8,128)S(1)} %collective-permute-done.24.l3, ...), custom_call_target="tpu_custom_call" | custom-call | tf_op jit(solution)/shard_map/pallas_call | solution.py:430
  190.5 15.5 %all_to_all.35 = f32[32,1,256]{2,1,0:T(1,128)S(1)} all-to-all(f32[32,1,256]{2,1,0:T(1,128)S(1)} %copy.24), channel_id=1, replica_groups=mesh['x'=4,'z'=8,'core'=2,'rep'=4] {'x','z'}, dimensions={0} | all-to-all | bytes 65536 | tf_op jit(solution)/shard_map/all_to_all | solution.py:440
  206.1 0.7 shard_map.97
  (38 shorter events, 0.2 us)
Async XLA Ops:
  0.6 48.1 %collective-permute-start.2 = (bf16[8,512,256]{2,1,0:T(8,128)(2,1)}, bf16[8,512,256]{2,1,0:T(8,128)(2,1)S(1)}, u32[]{:S(2)}, u32[]{:S(2)}) collective-permute-start(bf16[8,512,256]{2,1,0:T(8,128)(2,1)} %own.1), channel_id=1, source_target_pairs={{0,4},{4,0},{1,5},{5,1},{2,6},{6,2},{3,7},{7,3},{8,12},{12,8},{9,1... | collective-permute-start | bytes 6291464 | tf_op jit(solution)/shard_map/ppermute | solution.py:315
  4.0 10.2 %collective-permute-start.1 = (bf16[4,128,256]{2,1,0:T(8,128)(2,1)}, bf16[4,128,256]{2,1,0:T(8,128)(2,1)S(1)}, u32[]{:S(2)}, u32[]{:S(2)}) collective-permute-start(bf16[4,128,256]{2,1,0:T(8,128)(2,1)} %refs_0_.3), channel_id=1, source_target_pairs={{0,56},{8,0},{16,8},{24,16},{32,24},{40,32},{48,40},{56,48},{1,57}... | collective-permute-start | bytes 786440 | tf_op jit(solution)/shard_map/ppermute | solution.py:315
  7.8 9.0 %collective-permute-start = (bf16[4,128,256]{2,1,0:T(8,128)(2,1)}, bf16[4,128,256]{2,1,0:T(8,128)(2,1)S(1)}, u32[]{:S(2)}, u32[]{:S(2)}) collective-permute-start(bf16[4,128,256]{2,1,0:T(8,128)(2,1)} %refs_0_.3), channel_id=1, source_target_pairs={{0,8},{8,16},{16,24},{24,32},{32,40},{40,48},{48,56},{56,0},{1,9},... | collective-permute-start | bytes 786440 | tf_op jit(solution)/shard_map/ppermute | solution.py:315
  16.8 8.0 %collective-permute-start.3 = (bf16[4,128,256]{2,1,0:T(8,128)(2,1)S(1)}, bf16[4,128,256]{2,1,0:T(8,128)(2,1)S(1)}, u32[]{:S(2)}, u32[]{:S(2)}) collective-permute-start(bf16[4,128,256]{2,1,0:T(8,128)(2,1)S(1)} %collective-permute-done.refs_1_), channel_id=1, source_target_pairs={{0,8},{8,16},{16,24},{24,32},{32,40},{40,48},{48,56},{56,0},{1,9},... | collective-permute-start | bytes 786440 | tf_op jit(solution)/shard_map/ppermute | solution.py:315
  16.8 8.0 %collective-permute-start.5 = (bf16[4,128,256]{2,1,0:T(8,128)(2,1)S(1)}, bf16[4,128,256]{2,1,0:T(8,128)(2,1)S(1)}, u32[]{:S(2)}, u32[]{:S(2)}) collective-permute-start(bf16[4,128,256]{2,1,0:T(8,128)(2,1)S(1)} %collective-permute-done.1.refs_2_), channel_id=1, source_target_pairs={{0,56},{8,0},{16,8},{24,16},{32,24},{40,32},{48,40},{56,48},{1,57}... | collective-permute-start | bytes 786440 | tf_op jit(solution)/shard_map/ppermute | solution.py:315
  19.4 0.9 copy-start
  22.0 6.3 %collective-permute-start.11 = (bf16[2,128,256]{2,1,0:T(8,128)(2,1)S(1)}, bf16[2,128,256]{2,1,0:T(8,128)(2,1)S(1)}, u32[]{:S(2)}, u32[]{:S(2)}) collective-permute-start(bf16[2,128,256]{2,1,0:T(8,128)(2,1)S(1)} %get-tuple-element.49), channel_id=1, source_target_pairs={{0,64},{64,128},{128,192},{192,0},{1,65},{65,129},{129,193},{193,1... | collective-permute-start | bytes 393224 | tf_op jit(solution)/shard_map/ppermute | solution.py:315
  23.3 5.0 %collective-permute-start.12 = (bf16[2,128,256]{2,1,0:T(8,128)(2,1)S(1)}, bf16[2,128,256]{2,1,0:T(8,128)(2,1)S(1)}, u32[]{:S(2)}, u32[]{:S(2)}) collective-permute-start(bf16[2,128,256]{2,1,0:T(8,128)(2,1)S(1)} %get-tuple-element.50), channel_id=1, source_target_pairs={{0,192},{64,0},{128,64},{192,128},{1,193},{65,1},{129,65},{193,129... | collective-permute-start | bytes 393224 | tf_op jit(solution)/shard_map/ppermute | solution.py:315
  24.7 10.4 %collective-permute-start.4 = (bf16[4,128,256]{2,1,0:T(8,128)(2,1)S(1)}, bf16[4,128,256]{2,1,0:T(8,128)(2,1)S(1)}, u32[]{:S(2)}, u32[]{:S(2)}) collective-permute-start(bf16[4,128,256]{2,1,0:T(8,128)(2,1)S(1)} %collective-permute-done.3.refs_3_), channel_id=1, source_target_pairs={{0,8},{8,16},{16,24},{24,32},{32,40},{40,48},{48,56},{56,0},{1,9},... | collective-permute-start | bytes 786440 | tf_op jit(solution)/shard_map/ppermute | solution.py:315
  28.3 0.7 copy-start.5
  28.9 16.3 %collective-permute-start.13 = (bf16[8,128,256]{2,1,0:T(8,128)(2,1)S(1)}, bf16[8,128,256]{2,1,0:T(8,128)(2,1)S(1)}, u32[]{:S(2)}, u32[]{:S(2)}) collective-permute-start(bf16[8,128,256]{2,1,0:T(8,128)(2,1)S(1)} %get-tuple-element.55), channel_id=1, source_target_pairs={{0,64},{64,128},{128,192},{192,0},{1,65},{65,129},{129,193},{193,1... | collective-permute-start | bytes 1572872 | tf_op jit(solution)/shard_map/ppermute | solution.py:315
  30.0 6.0 %collective-permute-start.6 = (bf16[4,128,256]{2,1,0:T(8,128)(2,1)S(1)}, bf16[4,128,256]{2,1,0:T(8,128)(2,1)S(1)}, u32[]{:S(2)}, u32[]{:S(2)}) collective-permute-start(bf16[4,128,256]{2,1,0:T(8,128)(2,1)S(1)} %collective-permute-done.5.refs_4_), channel_id=1, source_target_pairs={{0,56},{8,0},{16,8},{24,16},{32,24},{40,32},{48,40},{56,48},{1,57}... | collective-permute-start | bytes 786440 | tf_op jit(solution)/shard_map/ppermute | solution.py:315
  32.7 33.1 %collective-permute-start.15 = (bf16[10,128,256]{2,1,0:T(8,128)(2,1)}, bf16[10,128,256]{2,1,0:T(8,128)(2,1)S(1)}, u32[]{:S(2)}, u32[]{:S(2)}) collective-permute-start(bf16[10,128,256]{2,1,0:T(8,128)(2,1)} %get-tuple-element.57), channel_id=1, source_target_pairs={{0,128},{64,192},{128,0},{192,64},{1,129},{65,193},{129,1},{193,65... | collective-permute-start | bytes 1966088 | tf_op jit(solution)/shard_map/ppermute | solution.py:315
  35.1 6.7 %collective-permute-start.7 = (bf16[4,128,256]{2,1,0:T(8,128)(2,1)S(1)}, bf16[4,128,256]{2,1,0:T(8,128)(2,1)S(1)}, u32[]{:S(2)}, u32[]{:S(2)}) collective-permute-start(bf16[4,128,256]{2,1,0:T(8,128)(2,1)S(1)} %collective-permute-done.4.refs_0_), channel_id=1, source_target_pairs={{0,8},{8,16},{16,24},{24,32},{32,40},{40,48},{48,56},{56,0},{1,9},... | collective-permute-start | bytes 786440 | tf_op jit(solution)/shard_map/ppermute | solution.py:315
  36.0 24.6 %collective-permute-start.14 = (bf16[8,128,256]{2,1,0:T(8,128)(2,1)}, bf16[8,128,256]{2,1,0:T(8,128)(2,1)}, u32[]{:S(2)}, u32[]{:S(2)}) collective-permute-start(bf16[8,128,256]{2,1,0:T(8,128)(2,1)} %get-tuple-element.56), channel_id=1, source_target_pairs={{0,192},{64,0},{128,64},{192,128},{1,193},{65,1},{129,65},{193,129... | collective-permute-start | bytes 1572872 | tf_op jit(solution)/shard_map/ppermute | solution.py:315
  44.5 0.7 copy-start.3
  45.2 27.7 %collective-permute-start.8 = (bf16[6,128,256]{2,1,0:T(8,128)(2,1)}, bf16[6,128,256]{2,1,0:T(8,128)(2,1)}, u32[]{:S(2)}, u32[]{:S(2)}) collective-permute-start(bf16[6,128,256]{2,1,0:T(8,128)(2,1)} %get-tuple-element.41), channel_id=1, source_target_pairs={{0,64},{64,128},{128,192},{192,0},{1,65},{65,129},{129,193},{193,1... | collective-permute-start | bytes 1179656 | tf_op jit(solution)/shard_map/ppermute | solution.py:315
  45.2 0.8 copy-start.1
  46.0 26.9 %collective-permute-start.9 = (bf16[6,128,256]{2,1,0:T(8,128)(2,1)}, bf16[6,128,256]{2,1,0:T(8,128)(2,1)}, u32[]{:S(2)}, u32[]{:S(2)}) collective-permute-start(bf16[6,128,256]{2,1,0:T(8,128)(2,1)} %get-tuple-element.42), channel_id=1, source_target_pairs={{0,192},{64,0},{128,64},{192,128},{1,193},{65,1},{129,65},{193,129... | collective-permute-start | bytes 1179656 | tf_op jit(solution)/shard_map/ppermute | solution.py:315
  48.7 24.4 %collective-permute-start.10 = (bf16[6,128,256]{2,1,0:T(8,128)(2,1)}, bf16[6,128,256]{2,1,0:T(8,128)(2,1)}, u32[]{:S(2)}, u32[]{:S(2)}) collective-permute-start(bf16[6,128,256]{2,1,0:T(8,128)(2,1)} %get-tuple-element.43), channel_id=1, source_target_pairs={{0,128},{64,192},{128,0},{192,64},{1,129},{65,193},{129,1},{193,65... | collective-permute-start | bytes 1179656 | tf_op jit(solution)/shard_map/ppermute | solution.py:315
  52.3 8.2 %copy-start.7 = (f32[8,512]{1,0:T(8,128)S(1)}, f32[8,512]{1,0:T(8,128)}, u32[]{:S(2)}) copy-start(f32[8,512]{1,0:T(8,128)} %log_a.3) | copy-start | bytes 49156
  52.3 13.5 %copy-start.2 = (bf16[8,128,256]{2,1,0:T(8,128)(2,1)S(1)}, bf16[8,128,256]{2,1,0:T(8,128)(2,1)}, u32[]{:S(2)}) copy-start(bf16[8,128,256]{2,1,0:T(8,128)(2,1)} %copy-done.1) | copy-start | bytes 1572868
  52.3 13.5 %copy-start.6 = (bf16[2,128,256]{2,1,0:T(8,128)(2,1)S(1)}, bf16[2,128,256]{2,1,0:T(8,128)(2,1)}, u32[]{:S(2)}) copy-start(bf16[2,128,256]{2,1,0:T(8,128)(2,1)} %copy-done.5) | copy-start | bytes 393220
  54.0 19.1 %copy-start.4 = (bf16[6,128,256]{2,1,0:T(8,128)(2,1)S(1)}, bf16[6,128,256]{2,1,0:T(8,128)(2,1)}, u32[]{:S(2)}) copy-start(bf16[6,128,256]{2,1,0:T(8,128)(2,1)} %copy-done.3) | copy-start | bytes 1179652
  60.6 12.3 %collective-permute-start.16 = (f32[8,512]{1,0:T(8,128)S(1)}, f32[8,512]{1,0:T(8,128)S(1)}, u32[]{:S(2)}, u32[]{:S(2)}) collective-permute-start(f32[8,512]{1,0:T(8,128)S(1)} %copy-done.7), channel_id=1, source_target_pairs={{0,4},{4,0},{1,5},{5,1},{2,6},{6,2},{3,7},{7,3},{8,12},{12,8},{9,1... | collective-permute-start | bytes 49160 | tf_op jit(solution)/shard_map/ppermute | solution.py:315
  87.5 2.9 %collective-permute-start.17 = (f32[16,512]{1,0:T(8,128)S(1)}, f32[16,512]{1,0:T(8,128)S(1)}, u32[]{:S(2)}, u32[]{:S(2)}) collective-permute-start(f32[16,512]{1,0:T(8,128)S(1)} %get-tuple-element.62), channel_id=1, source_target_pairs={{0,4},{4,0},{1,5},{5,1},{2,6},{6,2},{3,7},{7,3},{8,12},{12,8},{9,1... | collective-permute-start | bytes 98312 | tf_op jit(solution)/shard_map/ppermute | solution.py:315
  90.4 2.8 %collective-permute-start.20 = (f32[16,512]{1,0:T(8,128)S(1)}, f32[16,512]{1,0:T(8,128)S(1)}, u32[]{:S(2)}, u32[]{:S(2)}) collective-permute-start(f32[16,512]{1,0:T(8,128)S(1)} %log_add_fusion.1.l0), channel_id=1, source_target_pairs={{0,3},{1,0},{2,1},{3,2},{4,7},{5,4},{6,5},{7,6},{8,11},{9,8},{10,9... | collective-permute-start | bytes 98312 | tf_op jit(solution)/shard_map/ppermute | solution.py:315
  90.5 4.4 %collective-permute-start.19 = (f32[16,512]{1,0:T(8,128)S(1)}, f32[16,512]{1,0:T(8,128)S(1)}, u32[]{:S(2)}, u32[]{:S(2)}) collective-permute-start(f32[16,512]{1,0:T(8,128)S(1)} %log_add_fusion.1.l0), channel_id=1, source_target_pairs={{0,2},{1,3},{2,0},{3,1},{4,6},{5,7},{6,4},{7,5},{8,10},{9,11},{10,... | collective-permute-start | bytes 98312 | tf_op jit(solution)/shard_map/ppermute | solution.py:315
  90.6 5.4 %collective-permute-start.18 = (f32[16,512]{1,0:T(8,128)S(1)}, f32[16,512]{1,0:T(8,128)S(1)}, u32[]{:S(2)}, u32[]{:S(2)}) collective-permute-start(f32[16,512]{1,0:T(8,128)S(1)} %log_add_fusion.1.l0), channel_id=1, source_target_pairs={{0,1},{1,2},{2,3},{3,0},{4,5},{5,6},{6,7},{7,4},{8,9},{9,10},{10,1... | collective-permute-start | bytes 98312 | tf_op jit(solution)/shard_map/ppermute | solution.py:315
  96.0 37.3 %copy-start.8 = (f32[4,128]{1,0:T(4,128)S(1)}, f32[4,128]{1,0:T(4,128)}, u32[]{:S(2)}) copy-start(f32[4,128]{1,0:T(4,128)} %log_b.3) | copy-start | bytes 6148
  158.4 8.5 %collective-permute-start.21 = (f32[16,512]{1,0:T(8,128)S(1)}, f32[16,512]{1,0:T(8,128)S(1)}, u32[]{:S(2)}, u32[]{:S(2)}) collective-permute-start(f32[16,512]{1,0:T(8,128)S(1)} %shard_map.95), channel_id=1, source_target_pairs={{0,4},{4,0},{1,5},{5,1},{2,6},{6,2},{3,7},{7,3},{8,12},{12,8},{9,1... | collective-permute-start | bytes 98312 | tf_op jit(solution)/shard_map/ppermute | solution.py:315
  167.0 2.8 %collective-permute-start.24 = (f32[16,512]{1,0:T(8,128)S(1)}, f32[16,512]{1,0:T(8,128)S(1)}, u32[]{:S(2)}, u32[]{:S(2)}) collective-permute-start(f32[16,512]{1,0:T(8,128)S(1)} %log_add_fusion.l0), channel_id=1, source_target_pairs={{0,3},{1,0},{2,1},{3,2},{4,7},{5,4},{6,5},{7,6},{8,11},{9,8},{10,9... | collective-permute-start | bytes 98312 | tf_op jit(solution)/shard_map/ppermute | solution.py:315
  167.1 4.4 %collective-permute-start.23 = (f32[16,512]{1,0:T(8,128)S(1)}, f32[16,512]{1,0:T(8,128)S(1)}, u32[]{:S(2)}, u32[]{:S(2)}) collective-permute-start(f32[16,512]{1,0:T(8,128)S(1)} %log_add_fusion.l0), channel_id=1, source_target_pairs={{0,2},{1,3},{2,0},{3,1},{4,6},{5,7},{6,4},{7,5},{8,10},{9,11},{10,... | collective-permute-start | bytes 98312 | tf_op jit(solution)/shard_map/ppermute | solution.py:315
  167.2 5.4 %collective-permute-start.22 = (f32[16,512]{1,0:T(8,128)S(1)}, f32[16,512]{1,0:T(8,128)S(1)}, u32[]{:S(2)}, u32[]{:S(2)}) collective-permute-start(f32[16,512]{1,0:T(8,128)S(1)} %log_add_fusion.l0), channel_id=1, source_target_pairs={{0,1},{1,2},{2,3},{3,0},{4,5},{5,6},{6,7},{7,4},{8,9},{9,10},{10,1... | collective-permute-start | bytes 98312 | tf_op jit(solution)/shard_map/ppermute | solution.py:315
